TPU v7x, 256 devices: a whole 4x4x8 slice. The times are simulated.
256 devices in a mesh: tm: 16 (over z_hi, y), tensor: 8 (over x, core), dp: 2 (over z_lo).
Axes of the slice: x: 4, y: 4, z: 8 (z_hi: 4, z_lo: 2; z = z_hi * 2 + z_lo), core: 2. Of those that a mesh axis runs over, the one named last changes fastest.
Arguments:
- inputs: bfloat16 [2, 16384, 1536], P('dp', 'tm'), may hold values from -6 to 6
- grad_blocks: bfloat16 [2, 1024, 128, 1536], P('dp', 'tm', 'tensor'), may hold values from -6 to 6
- block_device: int32 [2, 1024, 1], P('dp'), may hold values from 0 to 15; in each aligned block of 64 rows (0 to 63, 64 to 127, ..., all dimensions but the last counted through in order) at most 5 rows name the same one
- block_sub: int32 [2, 1024], P('dp'), may hold values from 0 to 7
- block_rows: int32 [2, 1024], P('dp'), may hold values from 1 to 128
- seg_lengths: int32 [2, 22], P('dp'), may hold values from 1 to 750, 16384 in all within a row
- value_weight: bfloat16 [1536, 1536], P('tensor'), may hold values from -0.15625 to 0.15625
- gate_weight: bfloat16 [1536, 1536], P('tensor'), may hold values from -0.15625 to 0.15625
- out_weight: bfloat16 [1536, 1536], P('tensor'), may hold values from -0.15625 to 0.15625
- conv_kernel: bfloat16 [31, 1536], P(None, 'tensor'), may hold values from -1 to 1
- norm_gain: float32 [1536], replicated, may hold values from 0.5 to 1.5
Outputs:
- input_grad: bfloat16 [2, 16384, 1536], P('dp', ('tm', 'tensor'))
- value_grad: float32 [1536, 1536], P('tensor', ('tm', 'dp'))
- gate_grad: float32 [1536, 1536], P('tensor', ('tm', 'dp'))
- out_grad: float32 [1536, 1536], P('tensor', ('tm', 'dp'))
- kernel_grad: float32 [31, 1536], P(None, 'tensor')
- gain_grad: float32 [1536], replicated
Inputs may be any that keep to these rules, and one draw needn't show every extreme that they name: `block_device`: for each group and tm index t, among the 64 blocks t * 64 to (t + 1) * 64 - 1 no value appears more than 5 times; in some of these runs a value appears exactly 5 times. `seg_lengths`: the 22 lengths of each group sum to 16384; the largest is 750.
All inputs are finite; a program needn't handle non-finite values.
Results may differ from a plain program's by a relative error of at most 0.03.
Values may be sent and summed in bfloat16 or wider, within the bound.
A program may use at most 128 MiB of HBM per device.

v0:
```python
import math

import jax
import jax.numpy as jnp
from jax import lax
from jax.sharding import PartitionSpec as P

KERNEL = 31
ROWS_BLK = 128


epsilon = 1e-05


def with_halo(cells, sides, width):
    for axis, dim in sides:
        count = lax.axis_size(axis)
        ends = count - 1
        head = lax.slice_in_dim(cells, 0, width, axis=dim)
        tail = lax.slice_in_dim(cells, cells.shape[dim] - width, cells.shape[dim], axis=dim)
        cells = jnp.concatenate(
            [
                lax.ppermute(tail, axis, [(i, (i + 1) % count) for i in range(ends)]),
                cells,
                lax.ppermute(head, axis, [((i + 1) % count, i) for i in range(ends)]),
            ],
            axis=dim,
        )
    return cells


def segment_of(lengths, first, count, total):
    position = first + jnp.arange(count, dtype=jnp.int32)
    bounds = jnp.cumsum(lengths)
    labels = jnp.sum((position[:, None] >= bounds[None, :]).astype(jnp.int32), axis=1)
    inside = (position >= 0) & (position < total)
    return jnp.where(inside, labels, -1)


def contract_last(left, right):
    return lax.dot_general(
        left, right, (((1,), (1,)), ((), ())), preferred_element_type=jnp.float32
    )


def norm_backward(full_cot, norm_cot, normed, inv_std, norm_gain):
    scaled_cot = norm_cot * norm_gain
    return full_cot.astype(jnp.float32) + inv_std * (
        scaled_cot
        - jnp.mean(scaled_cot, axis=1, keepdims=True)
        - normed * jnp.mean(scaled_cot * normed, axis=1, keepdims=True)
    )


def on_device(
    inputs,
    grad_blocks,
    block_device,
    block_sub,
    block_rows,
    seg_lengths,
    value_weight,
    gate_weight,
    out_weight,
    conv_kernel,
    norm_gain,
):
    frames_in = inputs[0]
    tok_count, width = frames_in.shape
    span = value_weight.shape[0]
    half = KERNEL // 2
    tm_count = lax.axis_size("tm")
    tm_index = lax.axis_index("tm")
    frame_total = tok_count * tm_count
    factor = 1.0 / math.sqrt(lax.axis_size("dp") * frame_total)
    blocks = grad_blocks[0]
    blk_count, row_share = (blocks.shape[0], blocks.shape[1])
    per_dev = tok_count // ROWS_BLK
    capacity = max(2, (blk_count + tm_count - 1) // tm_count + 1)
    devices = block_device[0, :, 0].reshape(tm_count, blk_count)
    subs = block_sub[0].reshape(tm_count, blk_count)
    counts = block_rows[0].reshape(tm_count, blk_count)
    own_counts = lax.dynamic_index_in_dim(counts, tm_index, 0, keepdims=False)
    own_device = lax.dynamic_index_in_dim(devices, tm_index, 0, keepdims=False)
    row_ids = lax.axis_index("tensor") * row_share + jnp.arange(row_share, dtype=jnp.int32)
    live_rows = (row_ids[None, :] < own_counts[:, None]).astype(jnp.bfloat16)
    flat_blocks = (blocks * live_rows[:, :, None]).reshape(blk_count, row_share * width)
    earlier = jnp.arange(blk_count)[:, None] > jnp.arange(blk_count)[None, :]
    same_dest = devices[:, :, None] == devices[:, None, :]
    ranks = jnp.sum((same_dest & earlier[None, :, :]).astype(jnp.int32), axis=2)
    own_rank = lax.dynamic_index_in_dim(ranks, tm_index, 0, keepdims=False)
    slot = own_device * capacity + own_rank
    placing = (jnp.arange(tm_count * capacity)[:, None] == slot[None, :]).astype(jnp.bfloat16)
    outgoing = jnp.dot(placing, flat_blocks, preferred_element_type=jnp.float32).astype(
        jnp.bfloat16
    )
    outgoing = outgoing.reshape(tm_count, capacity, row_share, width)
    incoming = lax.all_to_all(outgoing, "tm", split_axis=0, concat_axis=0, tiled=True)
    mine = (devices == tm_index).astype(jnp.float32)
    rank_hot = (ranks[:, :, None] == jnp.arange(capacity)[None, None, :]).astype(jnp.float32)
    sub_hot = (subs[:, :, None] == jnp.arange(per_dev)[None, None, :]).astype(jnp.float32)
    assign = jnp.einsum("sb,sbc,sbq->qsc", mine, rank_hot, sub_hot).astype(jnp.bfloat16)
    assign = assign.reshape(per_dev, tm_count * capacity)
    gathered = jnp.dot(
        assign,
        incoming.reshape(tm_count * capacity, row_share * width),
        preferred_element_type=jnp.float32,
    )
    out_cot = gathered.reshape(per_dev, row_share, width).astype(jnp.bfloat16)
    frames_f32 = frames_in.astype(jnp.float32)
    centered = frames_f32 - jnp.mean(frames_f32, axis=1, keepdims=True)
    inv_std = lax.rsqrt(jnp.mean(centered * centered, axis=1, keepdims=True) + epsilon)
    normed = centered * inv_std
    norm_out = (normed * norm_gain).astype(jnp.bfloat16)
    value_lin = contract_last(norm_out, value_weight)
    gate_lin = contract_last(norm_out, gate_weight)
    gate_sig = jax.nn.sigmoid(gate_lin)
    glu_out = (value_lin * gate_sig).astype(jnp.bfloat16)
    labels = segment_of(
        seg_lengths[0], tm_index * tok_count - half, tok_count + 2 * half, frame_total
    )
    centre = labels[half : half + tok_count]
    near_masks = [
        (labels[offset : offset + tok_count] == centre).astype(jnp.float32)[:, None]
        for offset in range(KERNEL)
    ]
    glu_wide = with_halo(glu_out, (("tm", 0),), half).astype(jnp.float32)
    kern_f32 = conv_kernel.astype(jnp.float32)
    conv_out = jnp.zeros((tok_count, span), jnp.float32)
    for offset in range(KERNEL):
        conv_out = (
            conv_out + kern_f32[offset] * glu_wide[offset : offset + tok_count] * near_masks[offset]
        )
    conv_sig = jax.nn.sigmoid(conv_out)
    swish_out = (conv_out * conv_sig).astype(jnp.bfloat16)
    full_cot = lax.all_gather(out_cot, "tensor", axis=1, tiled=True).reshape(tok_count, width)
    out_term = jnp.dot(swish_out.T, full_cot, preferred_element_type=jnp.float32) * factor
    out_grad = lax.psum_scatter(
        out_term.astype(jnp.bfloat16), ("tm", "dp"), scatter_dimension=1, tiled=True
    ).astype(jnp.float32)
    swish_cot = contract_last(full_cot, out_weight)
    conv_cot = swish_cot * conv_sig * (1.0 + conv_out * (1.0 - conv_sig))
    cot_wide = with_halo(conv_cot, (("tm", 0),), half)
    glu_cot = jnp.zeros((tok_count, span), jnp.float32)
    kern_rows = []
    for offset in range(KERNEL):
        kern_rows.append(
            jnp.sum(conv_cot * glu_wide[offset : offset + tok_count] * near_masks[offset], axis=0)
        )
        mirror = KERNEL - 1 - offset
        glu_cot = (
            glu_cot + kern_f32[offset] * cot_wide[mirror : mirror + tok_count] * near_masks[mirror]
        )
    kern_part = jnp.stack(kern_rows) * factor
    value_cot = (glu_cot * gate_sig).astype(jnp.bfloat16)
    gate_cot = (glu_cot * value_lin * gate_sig * (1.0 - gate_sig)).astype(jnp.bfloat16)
    value_term = jnp.dot(value_cot.T, norm_out, preferred_element_type=jnp.float32) * factor
    gate_term = jnp.dot(gate_cot.T, norm_out, preferred_element_type=jnp.float32) * factor
    value_grad, gate_grad = (
        lax.psum_scatter(
            value_term.astype(jnp.bfloat16), ("tm", "dp"), scatter_dimension=1, tiled=True
        ).astype(jnp.float32),
        lax.psum_scatter(
            gate_term.astype(jnp.bfloat16), ("tm", "dp"), scatter_dimension=1, tiled=True
        ).astype(jnp.float32),
    )
    norm_cot = jnp.dot(value_cot, value_weight, preferred_element_type=jnp.float32) + jnp.dot(
        gate_cot, gate_weight, preferred_element_type=jnp.float32
    )
    summed_cot = lax.psum(norm_cot.astype(jnp.bfloat16), "tensor").astype(jnp.float32)
    gain_part = jnp.sum(summed_cot * normed, axis=0) * factor
    input_f32 = norm_backward(full_cot, summed_cot, normed, inv_std, norm_gain)
    share = tok_count // lax.axis_size("tensor")
    input_f32 = lax.dynamic_slice_in_dim(input_f32, lax.axis_index("tensor") * share, share, 0)
    kernel_grad, gain_grad = lax.psum((kern_part, gain_part), ("tm", "dp"))
    return (
        input_f32.astype(jnp.bfloat16)[None],
        value_grad,
        gate_grad,
        out_grad,
        kernel_grad,
        gain_grad,
    )


def solution(mesh):
    in_specs = (
        P("dp", "tm", None),
        P("dp", "tm", "tensor", None),
        P("dp", None, None),
        P("dp", None),
        P("dp", None),
        P("dp", None),
        P("tensor", None),
        P("tensor", None),
        P("tensor", None),
        P(None, "tensor"),
        P(),
    )
    out_specs = (
        P("dp", ("tm", "tensor"), None),
        P("tensor", ("tm", "dp")),
        P("tensor", ("tm", "dp")),
        P("tensor", ("tm", "dp")),
        P(None, "tensor"),
        P(),
    )
    return jax.shard_map(
        on_device, mesh=mesh, in_specs=in_specs, out_specs=out_specs, check_vma=False
    )
```

profile of v0, /device:TPU:0, one launch (start us, length us, event | category | flops | bytes accessed | tf_op | source)
XLA Modules:
  0.0 849.2 jit_solution(511970364349347830)
XLA Ops:
  16.4 3.3 copy.40
  19.7 9.6 %all-to-all-start = ((bf16[16,5,16,1536]{3,2,1,0:T(8,128)(2,1)}), bf16[16,5,16,1536]{3,2,1,0:T(8,128)(2,1)}, u32[]{:S(2)}, u32[]{:S(2)}) async-start(bf16[16,5,16,1536]{3,2,1,0:T(8,128)(2,1)} %bitcast.132), calls=%async_computation | async-start | bytes 7864320 | tf_op jit(solution)/shard_map/all_to_all | solution.py:98
  30.5 89.5 %all-to-all-done = bf16[16,5,16,1536]{3,2,1,0:T(8,128)(2,1)} async-done(((bf16[16,5,16,1536]{3,2,1,0:T(8,128)(2,1)}), bf16[16,5,16,1536]{3,2,1,0:T(8,128)(2,1)}, u32[]{:S(2)}, u32[]{:S(2)}) %all-to-all-start) | async-done | bytes 3932192 | tf_op jit(solution)/shard_map/all_to_all | solution.py:98
  120.0 7.1 fusion.12
  127.2 2.5 convert_reduce_fusion
  137.2 4.8 collective-permute-start
  144.0 8.9 %multiply_add_fusion = f32[1024,192]{0,1:T(8,128)} fusion(f32[1054,192]{0,1:T(8,128)S(1)} %convert_element_type.191, f32[1024]{0:T(1024)S(1)} %get-tuple-element.109, f32[192]{0:T(256)S(1)} %bitcast.201, f32[1024]{0:T(1024)S(1)} %get-tuple-element.82, f32[192]{0:T(256)S(1)} %bitcast.199, f32[1024]{0:T(1024)S(1)} %get-tuple-element.83, f32[192]{0:T(256)S(1)} %bitcast.197, ...), kind=kLoop, calls=%fused_computation.250 | loop fusion | flops 17891328 | bytes 25312512 | tf_op jit(solution)/shard_map/add | solution.py:132
  154.3 2.9 copy.34
  160.8 4.6 collective-permute-start.3
  165.4 2.2 fusion.11
  167.7 12.0 %multiply_convert_fusion.2 = (bf16[1024,192]{0,1:T(8,128)(2,1)}, f32[1024,192]{0,1:T(8,128)S(1)}) fusion(f32[1024,192]{0,1:T(8,128)S(1)} %fusion.19, f32[1024,192]{0,1:T(8,128)} %get-tuple-element.112, f32[1024]{0:T(1024)S(1)} %get-tuple-element.110, f32[1024,192]{0,1:T(8,128)S(1)} %get-tuple-element.113, f32[15,192]{0,1:T(8,128)S(1)} %collective-permute-done.3, ...), kind=kLoop, calls=%fused_computation.247 | loop fusion | flops 24772608 | bytes 3708672 | tf_op jit(solution)/shard_map/convert_element_type | solution.py:156
  179.9 2.3 fusion.9
  182.5 4.1 fusion.10
  187.8 2.7 add_convert_fusion
  191.3 2.4 multiply_reduce_fusion.2
  193.7 2.3 multiply_reduce_fusion.19
  196.0 2.3 multiply_reduce_fusion.1
  198.5 122.0 %reduce-scatter.8.cloned.1.call-done = bf16[192,48]{0,1:T(8,128)(2,1)} async-done(((bf16[192,1536]{0,1:T(8,128)(2,1)}), bf16[192,48]{0,1:T(8,128)(2,1)}) %reduce-scatter.8.cloned.1.call-update) | async-done | bytes 18448 | tf_op jit(solution)/shard_map/reduce_scatter | solution.py:138
  321.8 146.4 %reduce-scatter.4.cloned.1.call-done = bf16[192,48]{0,1:T(8,128)(2,1)} async-done(((bf16[192,1536]{0,1:T(8,128)(2,1)}), bf16[192,48]{0,1:T(8,128)(2,1)}) %reduce-scatter.4.cloned.1.call-update) | async-done | bytes 18448 | tf_op jit(solution)/shard_map/reduce_scatter | solution.py:160
  469.6 146.1 %reduce-scatter.6.cloned.1.call-done = bf16[192,48]{0,1:T(8,128)(2,1)} async-done(((bf16[192,1536]{0,1:T(8,128)(2,1)}), bf16[192,48]{0,1:T(8,128)(2,1)}) %reduce-scatter.6.cloned.1.call-update) | async-done | bytes 18448 | tf_op jit(solution)/shard_map/reduce_scatter | solution.py:163
  617.1 71.1 %all-reduce.3.cloned.1.call-done = bf16[1024,1536]{1,0:T(8,128)(2,1)} async-done(((bf16[1024,1536]{1,0:T(8,128)(2,1)}), bf16[1024,1536]{1,0:T(8,128)(2,1)}) %all-reduce.3.cloned.1.call-update) | async-done | bytes 3145744 | tf_op jit(solution)/shard_map/psum | solution.py:170
  688.2 8.3 fusion.4
  696.7 143.1 %all-reduce = (f32[31,192]{1,0:T(8,128)}, f32[1536]{0:T(1024)}) all-reduce(f32[31,192]{1,0:T(8,128)S(1)} %broadcast_multiply_fusion, f32[1536]{0:T(1024)S(1)} %broadcast_multiply_fusion.1), channel_id=1, replica_groups=mesh['tm'=16,'tensor'=8,'dp'=2] {'tm','dp'}, use_global_device_ids=true, to_apply=%region_42.43 | all-reduce | flops 7488 | bytes 59904 | tf_op jit(solution)/shard_map/psum | solution.py:175
  839.8 2.5 fusion.143
  (185 shorter events, 31.0 us)
Async XLA Ops:
  7.2 126.6 %copy-start = (bf16[192,1536]{1,0:T(8,128)(2,1)S(1)}, bf16[192,1536]{1,0:T(8,128)(2,1)}, u32[]{:S(2)}) copy-start(bf16[192,1536]{1,0:T(8,128)(2,1)} %param.17) | copy-start | bytes 1769476
  19.7 100.3 %all-to-all-start = ((bf16[16,5,16,1536]{3,2,1,0:T(8,128)(2,1)}), bf16[16,5,16,1536]{3,2,1,0:T(8,128)(2,1)}, u32[]{:S(2)}, u32[]{:S(2)}) async-start(bf16[16,5,16,1536]{3,2,1,0:T(8,128)(2,1)} %bitcast.132), calls=%async_computation | async-start | bytes 7864320 | tf_op jit(solution)/shard_map/all_to_all | solution.py:98
  29.4 124.9 %all-gather.2.cloned.1.call-start = ((), (), s32[]{:S(2)}) async-start(), calls=%async_computation.4 | async-start | bytes 3538944 | tf_op jit(solution)/shard_map/all_gather | solution.py:136
  127.1 193.3 %reduce-scatter.8.cloned.1.call-start = ((), (), s32[]{:S(2)}) async-start(), calls=%async_computation.8 | async-start | bytes 811008 | tf_op jit(solution)/shard_map/reduce_scatter | solution.py:138
  135.9 7.2 collective-permute-start.1
  137.2 6.3 collective-permute-start
  142.5 10.4 %copy-start.18 = (f32[1,192]{1,0:T(1,128)}, f32[1,192]{1,0:T(1,128)S(1)}, u32[]{:S(2)}) copy-start(f32[1,192]{1,0:T(1,128)S(1)} %get-tuple-element.50) | copy-start | bytes 2308
  142.5 10.4 %copy-start.19 = (f32[1,192]{1,0:T(1,128)}, f32[1,192]{1,0:T(1,128)S(1)}, u32[]{:S(2)}) copy-start(f32[1,192]{1,0:T(1,128)S(1)} %get-tuple-element.51) | copy-start | bytes 2308
  142.5 10.4 %copy-start.20 = (f32[1,192]{1,0:T(1,128)}, f32[1,192]{1,0:T(1,128)S(1)}, u32[]{:S(2)}) copy-start(f32[1,192]{1,0:T(1,128)S(1)} %get-tuple-element.52) | copy-start | bytes 2308
  142.5 10.4 %copy-start.21 = (f32[1,192]{1,0:T(1,128)}, f32[1,192]{1,0:T(1,128)S(1)}, u32[]{:S(2)}) copy-start(f32[1,192]{1,0:T(1,128)S(1)} %get-tuple-element.53) | copy-start | bytes 2308
  142.5 10.4 %copy-start.22 = (f32[1,192]{1,0:T(1,128)}, f32[1,192]{1,0:T(1,128)S(1)}, u32[]{:S(2)}) copy-start(f32[1,192]{1,0:T(1,128)S(1)} %get-tuple-element.54) | copy-start | bytes 2308
  142.5 10.4 %copy-start.23 = (f32[1,192]{1,0:T(1,128)}, f32[1,192]{1,0:T(1,128)S(1)}, u32[]{:S(2)}) copy-start(f32[1,192]{1,0:T(1,128)S(1)} %get-tuple-element.55) | copy-start | bytes 2308
  142.5 10.4 %copy-start.24 = (f32[1,192]{1,0:T(1,128)}, f32[1,192]{1,0:T(1,128)S(1)}, u32[]{:S(2)}) copy-start(f32[1,192]{1,0:T(1,128)S(1)} %get-tuple-element.56) | copy-start | bytes 2308
  142.6 10.4 %copy-start.25 = (f32[1,192]{1,0:T(1,128)}, f32[1,192]{1,0:T(1,128)S(1)}, u32[]{:S(2)}) copy-start(f32[1,192]{1,0:T(1,128)S(1)} %get-tuple-element.57) | copy-start | bytes 2308
  142.8 14.5 %copy-start.11 = (f32[1024]{0:T(1024)}, f32[1024]{0:T(1024)S(1)}, u32[]{:S(2)}) copy-start(f32[1024]{0:T(1024)S(1)} %get-tuple-element.90) | copy-start | bytes 12292
  142.8 14.4 %copy-start.12 = (f32[1024]{0:T(1024)}, f32[1024]{0:T(1024)S(1)}, u32[]{:S(2)}) copy-start(f32[1024]{0:T(1024)S(1)} %get-tuple-element.81) | copy-start | bytes 12292
  142.9 14.3 %copy-start.13 = (f32[1024]{0:T(1024)}, f32[1024]{0:T(1024)S(1)}, u32[]{:S(2)}) copy-start(f32[1024]{0:T(1024)S(1)} %get-tuple-element.99) | copy-start | bytes 12292
  159.5 8.2 collective-permute-start.2
  160.8 6.9 collective-permute-start.3
  167.7 300.6 %reduce-scatter.4.cloned.1.call-start = ((), (), s32[]{:S(2)}) async-start(), calls=%async_computation.6 | async-start | bytes 811008 | tf_op jit(solution)/shard_map/reduce_scatter | solution.py:160
  167.7 12.2 %copy-start.3 = (bf16[1024,1536]{1,0:T(8,128)(2,1)S(1)}, bf16[1024,1536]{1,0:T(8,128)(2,1)}, u32[]{:S(2)}) copy-start(bf16[1024,1536]{1,0:T(8,128)(2,1)} %copy-done.2) | copy-start | bytes 9437188
  182.2 433.5 %reduce-scatter.6.cloned.1.call-start = ((), (), s32[]{:S(2)}) async-start(), calls=%async_computation.7 | async-start | bytes 811008 | tf_op jit(solution)/shard_map/reduce_scatter | solution.py:163
  186.7 501.5 %all-reduce.3.cloned.1.call-start = ((), (), s32[]{:S(2)}) async-start(), calls=%async_computation.5 | async-start | bytes 6291456 | tf_op jit(solution)/shard_map/psum | solution.py:170
  196.0 492.2 %copy-start.17 = (f32[1536]{0:T(1024)S(1)}, f32[1536]{0:T(1024)}, u32[]{:S(2)}) copy-start(f32[1536]{0:T(1024)} %param.21) | copy-start | bytes 18436
  (42 other events, 302.6 us)
Sparse Core Ops, SparseCore 0:
  127.2 27.0 all-gather.1
  167.8 152.6 reduce-scatter.7
  323.1 145.0 reduce-scatter.3
  470.6 145.0 reduce-scatter.5
  618.1 70.1 all-reduce.2
where the time goes:
time: 856 us; the launch traced here: 849 us
  waiting for transfers between devices  577 us (67%)
  blocking collectives  143 us (17%)
  other arithmetic  52 us (6%)
  matrix products  26.2 us (3%)
  starting transfers between devices  22.2 us (3%)
  between operations  15.2 us (2%)
  local copies, waits for them, and re-layouts  13.7 us (2%)
    reduce_scatter x1, waiting for transfers between devices, on_device(): lax.psum_scatter(value_term.astype(jnp.bfloat16), ('tm', 'dp'), scatter_d...  146 us
    reduce_scatter x1, waiting for transfers between devices, on_device(): lax.psum_scatter(gate_term.astype(jnp.bfloat16), ('tm', 'dp'), scatter_di...  146 us
    psum x1, blocking collectives, on_device(): kernel_grad, gain_grad = lax.psum((kern_part, gain_part), ('tm', 'dp'))  143 us
    reduce_scatter x1, waiting for transfers between devices, on_device(): lax.psum_scatter(out_term.astype(jnp.bfloat16), ('tm', 'dp'), scatter_dim...  122 us
    all_to_all x1, waiting for transfers between devices, on_device(): lax.all_to_all(outgoing, 'tm', split_axis=0, concat_axis=0, tiled=True)  89.5 us
    psum x1, waiting for transfers between devices, on_device(): lax.psum(norm_cot.astype(jnp.bfloat16), 'tensor').astype(jnp.float32)  71.1 us
  transfers between devices with their start and end apart: 10, of which 7 were waited for; matrix products, arithmetic and copies ran while one was open for 6% of the time, Pallas kernels for 0%

commit v1 on v0

v1 whole, which is shorter than its diff:
```python
import math

import jax
import jax.numpy as jnp
from jax import lax
from jax.experimental import pallas as pl
from jax.experimental.pallas import tpu as pltpu
from jax.sharding import PartitionSpec as P

KERNEL = 31


epsilon = 1e-05


def contract_last(left, right):
    return lax.dot_general(
        left, right, (((1,), (1,)), ((), ())), preferred_element_type=jnp.float32
    )


def places():
    tm, te, dp = (lax.axis_index("tm"), lax.axis_index("tensor"), lax.axis_index("dp"))
    return tm, te, dp


def y_peer(step):
    tm, te, dp = places()
    return {"tm": (tm // 4) * 4 + (tm + step) % 4, "tensor": te, "dp": dp}


def z_peer(step):
    tm, te, dp = places()
    there = ((tm // 4) * 2 + dp + step) % 8
    return {"tm": (there // 2) * 4 + tm % 4, "tensor": te, "dp": there % 2}


def t_peer(step):
    tm, te, dp = places()
    return {"tm": tm, "tensor": (te + step) % 8, "dp": dp}


def x_peer(step):
    tm, te, dp = places()
    return {"tm": tm, "tensor": (te + 2 * step) % 8, "dp": dp}


def sibling():
    tm, te, dp = places()
    return {"tm": tm, "tensor": (te // 2) * 2 + 1 - te % 2, "dp": dp}


class Copies:
    def __init__(self, send_sems, recv_sems):
        self.send_sems, self.recv_sems = send_sems, recv_sems
        self.made = []

    def send(self, src, dst, to):
        at = len(self.made)
        copy = pltpu.make_async_remote_copy(
            src_ref=src,
            dst_ref=dst,
            send_sem=self.send_sems.at[at],
            recv_sem=self.recv_sems.at[at],
            device_id=to,
            device_id_type=pl.DeviceIdType.MESH,
        )
        copy.start()
        self.made.append(copy)
        return copy

    def finish(self):
        for copy in self.made:
            copy.wait_send()


def meet(peers):
    barrier = pltpu.get_barrier_semaphore()
    for peer in peers:
        pl.semaphore_signal(
            barrier, inc=1, device_id=peer, device_id_type=pl.DeviceIdType.MESH
        )
    pl.semaphore_wait(barrier, len(peers))


def f32(value):
    return value.astype(jnp.float32)


def frame_peer(step):
    tm, te, dp = places()
    return {"tm": (tm + step) % 16, "tensor": te, "dp": dp}


CHUNKS = ((0, 512), (512, 512), (1024, 256), (1280, 256))
HALVES = ((0, 768), (768, 768))
SLOTS = 320
COPIES = 13 * len(CHUNKS) + 4 + 7 * len(HALVES) + 12 + 14 + 7 + 3 + 7


def joint_kernel(
    table_ref,
    lengths_ref,
    frames_hbm,
    blocks_hbm,
    value_hbm,
    gate_hbm,
    out_hbm,
    taps_ref,
    gain_ref,
    input_grad,
    value_grad,
    gate_grad,
    out_grad,
    kernel_grad,
    gain_grad,
    frames_ref,
    pair_ref,
    last_ref,
    taps,
    ahead_ref,
    behind_ref,
    norm_ref,
    lin_ref,
    sig_ref,
    conv_ref,
    glu_0,
    glu_1,
    full_ref,
    swish_ref,
    cot_ref,
    cot_0,
    cot_1,
    both_cot,
    tap_sums,
    gain_sums,
    summing,
    edge_out,
    edge_in,
    far_out,
    far_in,
    part_ref,
    core_in,
    chip_sum,
    x_a,
    x_b,
    x_plus,
    x_minus,
    both_ref,
    both_a,
    both_b,
    both_plus,
    both_minus,
    both_mid,
    both_z,
    out_ref,
    out_a,
    out_b,
    out_plus,
    out_minus,
    out_mid,
    out_z,
    small_ref,
    gain_in,
    small_mid,
    small_y,
    small_last,
    small_z,
    load_sems,
    send_sems,
    recv_sems,
    *rest,
):
    count = len(CHUNKS)
    y_out, y_in = (rest[:count], rest[count : 2 * count])
    z_out, z_in = (rest[2 * count : 3 * count], rest[3 * count : 4 * count])
    blocks = rest[4 * count :]
    tm, te, dp = places()
    y, zh, z = (tm % 4, tm // 4, (tm // 4) * 2 + dp)
    x, core = (te // 2, te % 2)
    bf16 = jnp.bfloat16
    factor = 1.0 / math.sqrt(32768.0)
    columns = [pl.ds(first, size) for first, size in CHUNKS]

    loads = []

    def load(src, dst):
        copy = pltpu.make_async_copy(src, dst, load_sems.at[len(loads)])
        copy.start()
        loads.append(copy)
        return copy

    block_loads = [load(blocks_hbm.at[:, :, columns[c]], blocks[c]) for c in range(count)]
    frames_load = load(frames_hbm, frames_ref)
    weight_loads = [
        load(value_hbm.at[pl.ds(0, 128)], pair_ref.at[pl.ds(0, 128)]),
        load(gate_hbm.at[pl.ds(0, 128)], pair_ref.at[pl.ds(128, 128)]),
        load(value_hbm.at[pl.ds(128, 64)], pair_ref.at[pl.ds(256, 64)]),
        load(gate_hbm.at[pl.ds(128, 64)], pair_ref.at[pl.ds(320, 64)]),
    ]
    out_load = load(out_hbm, last_ref.at[pl.ds(0, 192)])

    meet(
        [t_peer(k) for k in range(1, 8)]
        + [y_peer(k) for k in range(1, 4)]
        + [z_peer(k) for k in range(1, 8)]
        + [frame_peer(1), frame_peer(-1)]
    )
    net = Copies(send_sems, recv_sems)

    def place(c):
        block_loads[c].wait()
        copies = []
        for k in (2, 1, 3, 0):
            first = ((y + k) % 4) * 20
            target = y_in[c].at[y] if k == 0 else y_out[c].at[k - 1]

            @pl.loop(0, 20)
            def _(slot):
                source = table_ref[first + slot]
                live = table_ref[80 + first + slot]
                rows = blocks[c][source]
                ids = lax.broadcasted_iota(jnp.int32, rows.shape, 0)
                target[pl.ds(pl.multiple_of(slot * 16, 16), 16)] = jnp.where(
                    ids < live, f32(rows), 0.0
                ).astype(bf16)

            if k:
                copies.append(net.send(target, y_in[c].at[y], y_peer(k)))
        return copies

    def combine(c, copies):
        for copy in copies:
            copy.wait_recv()
        width = CHUNKS[c][1]

        @pl.loop(0, width, step=256)
        def _(col):
            cols = pl.ds(pl.multiple_of(col, 256), 256)
            total = jnp.dot(
                summing[...],
                y_in[c][:, :, cols].reshape(4 * SLOTS, 256),
                preferred_element_type=jnp.float32,
            ).astype(bf16)
            for at in range(4):
                z_out[c][at, :, cols] = total[128 * at : 128 * at + 128]

        return [
            net.send(z_out[c].at[(zh + k) % 4], z_in[c].at[k - 1], z_peer(2 * k))
            for k in (2, 1, 3)
        ]

    def spread(c, copies):
        for copy in copies:
            copy.wait_recv()
        total = f32(z_out[c][zh])
        for k in range(3):
            total = total + f32(z_in[c][k])
        total = total.astype(bf16)
        for block in range(8):
            full_ref[block, te, :, columns[c]] = total[16 * block : 16 * block + 16]
        own = full_ref.at[:, te, :, columns[c]]
        return [net.send(own, own, x_peer(k)) for k in (2, 1, 3)], [
            net.send(own, own, sibling())
        ]

    def relay(c, copies):
        for k, copy in zip((2, 1, 3), copies[0]):
            copy.wait_recv()
            there = full_ref.at[:, (te + 8 - 2 * k) % 8, :, columns[c]]
            copies[1].append(net.send(there, there, sibling()))
        return copies[1]

    def project(c, copies):
        for copy in copies:
            copy.wait_recv()

        @pl.loop(0, 8, step=4)
        def _(block):
            rows = pl.ds(pl.multiple_of(block * 128, 512), 512)
            term = contract_last(
                full_ref[pl.ds(block, 4), :, :, columns[c]].reshape(512, CHUNKS[c][1]),
                last_ref[:, columns[c]],
            )
            if c == 0:
                cot_ref[rows] = term
            else:
                cot_ref[rows] += term

    y_copies = [place(0), place(1)]

    @pl.loop(0, 10)
    def _(group):
        tiles = []
        for k in range(8):
            at = table_ref[160 + group * 8 + k] * 16
            gap = lax.broadcasted_iota(jnp.int32, (16, 512), 1) - lax.broadcasted_iota(
                jnp.int32, (16, 512), 0
            )
            tiles.append(jnp.where(gap == at, 1.0, 0.0))
        cols = pl.ds(pl.multiple_of(group * 128, 128), 128)
        summing[:, cols] = jnp.concatenate(tiles, axis=0).T.astype(bf16)

    frames_load.wait()

    @pl.loop(0, 1024, step=32)
    def _(row):
        rows = pl.ds(pl.multiple_of(row, 32), 32)
        cells = f32(frames_ref[rows])
        centered = cells - jnp.mean(cells, axis=1, keepdims=True)
        scale = lax.rsqrt(jnp.mean(centered * centered, axis=1, keepdims=True) + epsilon)
        norm_ref[rows] = ((centered * scale) * gain_ref[...]).astype(bf16)

    for copy in weight_loads:
        copy.wait()

    @pl.loop(0, 1024, step=256)
    def _(row):
        rows = pl.ds(pl.multiple_of(row, 256), 256)
        wide = pl.ds(pl.multiple_of(row + 16, 16), 256)
        lin = contract_last(norm_ref[rows], pair_ref[...])
        value_0, gate_0, value_1 = (lin[:, :128], lin[:, 128:256], lin[:, 256:])
        sig_0 = jax.nn.sigmoid(gate_0)
        sig_1 = jax.nn.sigmoid(pltpu.roll(value_1, 64, 1))
        lin_ref[rows, :128] = value_0
        lin_ref[rows, 128:] = value_1
        sig_ref[rows, :128] = sig_0
        sig_ref[rows, 128:] = sig_1
        glu_0[wide] = f32((value_0 * sig_0).astype(bf16))
        glu_1[wide] = f32((value_1 * sig_1).astype(bf16))

    for at, first in ((0, 16), (1, 1024)):
        edge_out[at, :, :128] = glu_0[first : first + 16].astype(bf16)
        edge_out[at, :, 128:] = glu_1[first : first + 16].astype(bf16)
    edges = (
        net.send(edge_out.at[0], edge_in.at[1], frame_peer(-1)),
        net.send(edge_out.at[1], edge_in.at[0], frame_peer(1)),
    )

    z_copies = [combine(0, y_copies[0])]
    y_copies.append(place(2))

    taps[...] = jnp.zeros(taps.shape, jnp.float32)
    taps[:KERNEL, :192] = f32(taps_ref[...])
    last_ref[192:] = jnp.zeros((64, 1536), bf16)
    tap_sums[...] = jnp.zeros(tap_sums.shape, jnp.float32)
    ends = [lengths_ref[0, 0]]
    for at in range(1, 22):
        ends.append(ends[-1] + lengths_ref[0, at])

    @pl.loop(0, 1024, step=64)
    def _(row):
        rows = pl.ds(pl.multiple_of(row, 64), 64)
        at = lax.broadcasted_iota(jnp.int32, (64, 128), 0) + (tm * 1024 + row)
        end, start = (jnp.full((64, 128), 16384, jnp.int32), jnp.zeros((64, 128), jnp.int32))
        for bound in ends:
            past = at >= bound
            start = jnp.where(past, bound, start)
            end = jnp.where(past, end, jnp.minimum(end, bound))
        ahead_ref[rows] = end - 1 - at
        behind_ref[rows] = at - start

    for at, first in ((0, 0), (1, 1040)):
        edges[1 - at].wait_recv()
        glu_0[first : first + 16] = f32(edge_in[at, :, :128])
        glu_1[first : first + 16] = f32(edge_in[at, :, 128:])

    def nearby(ahead, behind, off):
        return ahead >= off if off > 0 else behind >= -off

    @pl.loop(0, 1024, step=32)
    def _(row):
        rows = pl.ds(pl.multiple_of(row, 32), 32)
        ahead, behind = (ahead_ref[rows], behind_ref[rows])
        total_0 = jnp.zeros((32, 128), jnp.float32)
        total_1 = jnp.zeros((32, 128), jnp.float32)
        for k in range(KERNEL):
            off = k - KERNEL // 2
            near = nearby(ahead, behind, off)
            shifted = pl.ds(row + 16 + off, 32)
            total_0 = total_0 + taps[k : k + 1, :128] * jnp.where(near, glu_0[shifted], 0.0)
            total_1 = total_1 + taps[k : k + 1, 128:] * jnp.where(near, glu_1[shifted], 0.0)
        conv_ref[rows, :128] = total_0
        conv_ref[rows, 128:] = total_1
        swish_ref[rows, :128] = (total_0 * jax.nn.sigmoid(total_0)).astype(bf16)
        swish_ref[rows, 128:] = (total_1 * jax.nn.sigmoid(total_1)).astype(bf16)

    out_load.wait()
    z_copies.append(combine(1, y_copies[1]))
    y_copies.append(place(3))
    x_copies = [spread(0, z_copies[0])]
    z_copies.append(combine(2, y_copies[2]))
    x_copies.append(spread(1, z_copies[1]))
    last = [relay(0, x_copies[0])]
    project(0, last[0])
    z_copies.append(combine(3, y_copies[3]))
    x_copies.append(spread(2, z_copies[2]))
    last.append(relay(1, x_copies[1]))
    project(1, last[1])
    x_copies.append(spread(3, z_copies[3]))
    last.append(relay(2, x_copies[2]))
    project(2, last[2])
    last.append(relay(3, x_copies[3]))
    project(3, last[3])

    @pl.loop(0, 1024, step=64)
    def _(row):
        rows = pl.ds(pl.multiple_of(row, 64), 64)
        wide = pl.ds(pl.multiple_of(row + 16, 16), 64)
        conv = conv_ref[rows]
        sig = jax.nn.sigmoid(conv)
        cot = cot_ref[rows] * sig * (1.0 + conv * (1.0 - sig))
        cot_0[wide] = cot[:, :128]
        cot_1[wide] = cot[:, 128:]

    for at, first in ((0, 16), (1, 1024)):
        far_out[at, :, :128] = cot_0[first : first + 16]
        far_out[at, :, 128:] = cot_1[first : first + 16]
    edges = (
        net.send(far_out.at[0], far_in.at[1], frame_peer(-1)),
        net.send(far_out.at[1], far_in.at[0], frame_peer(1)),
    )

    over_frames = (((0,), (0,)), ((), ()))
    lower, upper = (pl.ds(0, 2), pl.ds(2, 2))
    y_next, y_last, y_far = ((y + 1) % 4, (y + 3) % 4, (y + 2) % 4)
    x_next, x_last, x_far = ((x + 1) % 4, (x + 3) % 4, (x + 2) % 4)

    def begin_y(ref, a, b, plus, minus):
        first = (
            net.send(ref.at[lower, y_far], a, y_peer(1)),
            net.send(ref.at[upper, y_far], b, y_peer(-1)),
        )
        plain = (
            net.send(ref.at[upper, y_next], plus.at[upper], y_peer(1)),
            net.send(ref.at[lower, y_last], minus.at[lower], y_peer(-1)),
        )
        return first, plain

    def pass_y(begun, ref, a, b, plus, minus):
        first, plain = begun
        first[0].wait_recv()
        for i in range(2):
            a[i] = (f32(a[i]) + f32(ref[i, y_next])).astype(bf16)
        one = net.send(a, plus.at[lower], y_peer(1))
        first[1].wait_recv()
        for i in range(2):
            b[i] = (f32(b[i]) + f32(ref[i + 2, y_last])).astype(bf16)
        return plain + (one, net.send(b, minus.at[upper], y_peer(-1)))

    def begin_z(passed, ref, plus, minus, mid, z_in_ref):
        for copy in passed:
            copy.wait_recv()
        for i in range(4):
            total = (f32(ref[i, y]) + f32(plus[i]) + f32(minus[i])).astype(bf16)
            mid[2 * i] = total[:48]
            mid[2 * i + 1] = total[48:]
        z_in_ref[z] = mid[z]
        return [
            net.send(mid.at[(z + k) % 8], z_in_ref.at[z], z_peer(k)) for k in (4, 3, 5, 2, 6, 1, 7)
        ]

    def end_z(copies, z_in_ref):
        for copy in copies:
            copy.wait_recv()
        total = f32(z_in_ref[0])
        for at in range(1, 8):
            total = total + f32(z_in_ref[at])
        return total * factor

    @pl.loop(0, 4)
    def _(at):
        cols = pl.ds(pl.multiple_of(at * 384, 128), 384)
        term = lax.dot_general(
            full_ref[:, :, :, cols].reshape(1024, 384),
            swish_ref[...],
            over_frames,
            preferred_element_type=jnp.float32,
        ).astype(bf16)
        for k in range(4):
            out_ref[at, k] = term[96 * k : 96 * k + 96]

    out_set = (out_a, out_b, out_plus, out_minus)
    both_set = (both_a, both_b, both_plus, both_minus)
    out_begun = begin_y(out_ref, *out_set)

    for at, first in ((0, 0), (1, 1040)):
        edges[1 - at].wait_recv()
        cot_0[first : first + 16] = far_in[at, :, :128]
        cot_1[first : first + 16] = far_in[at, :, 128:]

    def back(row):
        rows = pl.ds(pl.multiple_of(row, 32), 32)
        wide = pl.ds(pl.multiple_of(row + 16, 16), 32)
        ahead, behind = (ahead_ref[rows], behind_ref[rows])
        here_0, here_1 = (cot_0[wide], cot_1[wide])
        total_0 = jnp.zeros((32, 128), jnp.float32)
        total_1 = jnp.zeros((32, 128), jnp.float32)
        for k in range(KERNEL):
            off = k - KERNEL // 2
            near = nearby(ahead, behind, off)
            shifted = pl.ds(row + 16 + off, 32)
            m = KERNEL - 1 - k
            total_0 = total_0 + taps[m : m + 1, :128] * jnp.where(near, cot_0[shifted], 0.0)
            total_1 = total_1 + taps[m : m + 1, 128:] * jnp.where(near, cot_1[shifted], 0.0)
            term_0 = here_0 * jnp.where(near, glu_0[shifted], 0.0)
            term_1 = here_1 * jnp.where(near, glu_1[shifted], 0.0)
            tap_sums[k, :, :128] += jnp.sum(term_0.reshape(4, 8, 128), axis=0)
            tap_sums[k, :, 128:] += jnp.sum(term_1.reshape(4, 8, 128), axis=0)
        value_0, value_1 = (lin_ref[rows, :128], lin_ref[rows, 128:])
        sig_0, sig_1 = (sig_ref[rows, :128], sig_ref[rows, 128:])
        both_cot[rows, :128] = (total_0 * sig_0).astype(bf16)
        both_cot[rows, 128:256] = (total_0 * value_0 * sig_0 * (1.0 - sig_0)).astype(bf16)
        gate_1 = total_1 * value_1 * sig_1 * (1.0 - sig_1)
        both_cot[rows, 256:] = (total_1 * sig_1 + pltpu.roll(gate_1, 64, 1)).astype(bf16)

    @pl.loop(0, 512, step=32)
    def _(row):
        back(row)

    out_passed = pass_y(out_begun, out_ref, *out_set)

    @pl.loop(512, 1024, step=32)
    def _(row):
        back(row)

    gain_sums[...] = jnp.zeros(gain_sums.shape, jnp.float32)
    core_copies = []
    for at, (first, size) in enumerate(HALVES):
        @pl.loop(first, first + size, step=256)
        def _(col):
            cols = pl.ds(pl.multiple_of(col, 256), 256)
            for row in (0, 512):
                part = jnp.dot(
                    both_cot[row : row + 512],
                    pair_ref[:, cols],
                    preferred_element_type=jnp.float32,
                )
                gain_sums[:, cols] += jnp.sum(
                    (part * f32(norm_ref[row : row + 512, cols])).reshape(64, 8, 256), axis=0
                )
                part = part.astype(bf16)
                for k in range(4):
                    part_ref[row // 256 + k // 2, k % 2, :, cols] = part[128 * k : 128 * k + 128]

        cols = pl.ds(first, size)
        core_copies.append(
            net.send(part_ref.at[:, 1 - core, :, cols], core_in.at[:, :, cols], sibling())
        )

    @pl.loop(0, 4)
    def _(at):
        cols = pl.ds(pl.multiple_of(at * 384, 128), 384)
        term = lax.dot_general(
            norm_ref[:, cols], both_cot[...], over_frames, preferred_element_type=jnp.float32
        ).astype(bf16)
        for k in range(4):
            both_ref[at, k] = term[96 * k : 96 * k + 96]

    both_begun = begin_y(both_ref, *both_set)

    gain_rows = pl.ds(32, 8)
    small_ref[...] = jnp.zeros(small_ref.shape, jnp.float32)
    for k in range(KERNEL):
        small_ref[k : k + 1] = jnp.sum(tap_sums[k], axis=0, keepdims=True)
    gain_part = jnp.sum(gain_sums[...], axis=0, keepdims=True) / gain_ref[...]
    for k in range(6):
        small_ref[32 + k : 33 + k] = gain_part[:, 256 * k : 256 * k + 256]
    gain_in[te] = small_ref[gain_rows, :]
    gain_copies = [
        net.send(small_ref.at[gain_rows], gain_in.at[te], t_peer(k)) for k in range(1, 8)
    ]

    half_a, half_b = (pl.ds(0, 64), pl.ds(64, 64))
    x_begun = []
    for at, (first, size) in enumerate(HALVES):
        core_copies[at].wait_recv()
        cols = pl.ds(first, size)

        def add_core(to):
            @pl.loop(0, 128, step=32)
            def _(row):
                rows = pl.ds(pl.multiple_of(row, 32), 32)
                chip_sum[to, rows, cols] = (
                    f32(part_ref[to, core, rows, cols]) + f32(core_in[to, rows, cols])
                ).astype(bf16)

        add_core(x_far)
        begun = (
            net.send(chip_sum.at[x_far, half_a, cols], x_a.at[:, cols], x_peer(1)),
            net.send(chip_sum.at[x_far, half_b, cols], x_b.at[:, cols], x_peer(-1)),
        )
        add_core(x_next)
        add_core(x_last)
        plain = (
            net.send(chip_sum.at[x_next, half_b, cols], x_plus.at[half_b, cols], x_peer(1)),
            net.send(chip_sum.at[x_last, half_a, cols], x_minus.at[half_a, cols], x_peer(-1)),
        )
        x_begun.append((begun, plain))

    out_z_copies = begin_z(out_passed, out_ref, out_plus, out_minus, out_mid, out_z)
    both_passed = pass_y(both_begun, both_ref, *both_set)

    x_passed = []
    for at, (first, size) in enumerate(HALVES):
        begun, plain = x_begun[at]
        cols = pl.ds(first, size)

        def add_x(ref, to, start):
            @pl.loop(0, 64, step=32)
            def _(row):
                rows = pl.ds(pl.multiple_of(row, 32), 32)
                other = pl.ds(pl.multiple_of(row + start, 32), 32)
                ref[rows, cols] = (f32(ref[rows, cols]) + f32(chip_sum[to, other, cols])).astype(
                    bf16
                )

        begun[0].wait_recv()
        add_x(x_a, x_next, 0)
        one = net.send(x_a.at[:, cols], x_plus.at[half_a, cols], x_peer(1))
        begun[1].wait_recv()
        add_x(x_b, x_last, 64)
        x_passed.append(
            plain + (one, net.send(x_b.at[:, cols], x_minus.at[half_b, cols], x_peer(-1)))
        )

    for copy in gain_copies:
        copy.wait_recv()
    small_mid[pl.ds(0, 32), :] = small_ref[pl.ds(0, 32), :]
    total = gain_in[0]
    for at in range(1, 8):
        total = total + gain_in[at]
    small_mid[gain_rows, :] = total
    small_y[y] = small_mid[...]
    small_copies = [net.send(small_mid, small_y.at[y], y_peer(k)) for k in range(1, 4)]

    both_z_copies = begin_z(both_passed, both_ref, both_plus, both_minus, both_mid, both_z)

    for copy in small_copies:
        copy.wait_recv()
    total = small_y[0]
    for at in range(1, 4):
        total = total + small_y[at]
    small_last[...] = total
    small_z[z] = total
    last_copies = [net.send(small_last, small_z.at[z], z_peer(k)) for k in range(1, 8)]

    out_grad[...] = end_z(out_z_copies, out_z).T[:192]

    for copies in x_passed:
        for copy in copies:
            copy.wait_recv()

    @pl.loop(0, 8)
    def _(block):
        rows = pl.ds(pl.multiple_of(block * 16, 16), 16)
        summed = (
            f32(part_ref[x, core, rows])
            + f32(core_in[x, rows])
            + f32(x_plus[rows])
            + f32(x_minus[rows])
        )
        cells = f32(frames_ref[pl.ds(pl.multiple_of(te * 128 + block * 16, 16), 16)])
        centered = cells - jnp.mean(cells, axis=1, keepdims=True)
        inv_std = lax.rsqrt(jnp.mean(centered * centered, axis=1, keepdims=True) + epsilon)
        normed = centered * inv_std
        scaled = summed * gain_ref[...]
        input_grad[rows] = (
            f32(full_ref[te, block])
            + inv_std
            * (
                scaled
                - jnp.mean(scaled, axis=1, keepdims=True)
                - normed * jnp.mean(scaled * normed, axis=1, keepdims=True)
            )
        ).astype(bf16)

    both_sum = end_z(both_z_copies, both_z)
    tail = both_sum[:, 256:].T
    value_grad[:128] = both_sum[:, :128].T
    gate_grad[:128] = both_sum[:, 128:256].T
    value_grad[128:] = tail[:64]
    gate_grad[128:] = tail[64:]

    for copy in last_copies:
        copy.wait_recv()
    total = small_z[0]
    for at in range(1, 8):
        total = total + small_z[at]
    total = total * factor
    kernel_grad[...] = total[:KERNEL, :192]
    for k in range(6):
        gain_grad[:, 256 * k : 256 * k + 256] = total[32 + k : 33 + k]
    net.finish()


def joint_call(table, lengths, frames, blocks, value_weight, gate_weight, out_weight, taps, gain):
    count, width = frames.shape
    span = value_weight.shape[0]
    bf16, single = (jnp.bfloat16, jnp.float32)
    vmem = pl.BlockSpec(memory_space=pltpu.VMEM)
    smem = pl.BlockSpec(memory_space=pltpu.SMEM)
    where = pl.BlockSpec(memory_space=pl.ANY)

    def weight_scratch(lanes):
        return [
            pltpu.VMEM((4, 4, 96, lanes), bf16),
            pltpu.VMEM((2, 96, lanes), bf16),
            pltpu.VMEM((2, 96, lanes), bf16),
            pltpu.VMEM((4, 96, lanes), bf16),
            pltpu.VMEM((4, 96, lanes), bf16),
            pltpu.VMEM((8, 48, lanes), bf16),
            pltpu.VMEM((8, 48, lanes), bf16),
        ]

    return pl.pallas_call(
        joint_kernel,
        out_shape=(
            jax.ShapeDtypeStruct((128, width), bf16),
            jax.ShapeDtypeStruct((span, 48), single),
            jax.ShapeDtypeStruct((span, 48), single),
            jax.ShapeDtypeStruct((span, 48), single),
            jax.ShapeDtypeStruct((KERNEL, span), single),
            jax.ShapeDtypeStruct((1, width), single),
        ),
        in_specs=[smem, smem] + [where] * 5 + [vmem] * 2,
        out_specs=[vmem] * 6,
        scratch_shapes=[
            pltpu.VMEM((count, width), bf16),
            pltpu.VMEM((2 * span, width), bf16),
            pltpu.VMEM((256, width), bf16),
            pltpu.VMEM((32, 256), single),
            pltpu.VMEM((count, 128), jnp.int32),
            pltpu.VMEM((count, 128), jnp.int32),
            pltpu.VMEM((count, width), bf16),
            pltpu.VMEM((count, 256), single),
            pltpu.VMEM((count, 256), single),
            pltpu.VMEM((count, 256), single),
            pltpu.VMEM((count + 32, 128), single),
            pltpu.VMEM((count + 32, 128), single),
            pltpu.VMEM((8, 8, 16, width), bf16),
            pltpu.VMEM((count, 256), bf16),
            pltpu.VMEM((count, 256), single),
            pltpu.VMEM((count + 32, 128), single),
            pltpu.VMEM((count + 32, 128), single),
            pltpu.VMEM((count, 2 * span), bf16),
            pltpu.VMEM((KERNEL, 8, 256), single),
            pltpu.VMEM((8, width), single),
            pltpu.VMEM((512, 4 * SLOTS), bf16),
            pltpu.VMEM((2, 16, 256), bf16),
            pltpu.VMEM((2, 16, 256), bf16),
            pltpu.VMEM((2, 16, 256), single),
            pltpu.VMEM((2, 16, 256), single),
            pltpu.VMEM((4, 2, 128, width), bf16),
            pltpu.VMEM((4, 128, width), bf16),
            pltpu.VMEM((4, 128, width), bf16),
            pltpu.VMEM((64, width), bf16),
            pltpu.VMEM((64, width), bf16),
            pltpu.VMEM((128, width), bf16),
            pltpu.VMEM((128, width), bf16),
        ]
        + weight_scratch(2 * span)
        + weight_scratch(256)
        + [
            pltpu.VMEM((40, 256), single),
            pltpu.VMEM((8, 8, 256), single),
            pltpu.VMEM((40, 256), single),
            pltpu.VMEM((4, 40, 256), single),
            pltpu.VMEM((40, 256), single),
            pltpu.VMEM((8, 40, 256), single),
            pltpu.SemaphoreType.DMA((len(CHUNKS) + 6,)),
            pltpu.SemaphoreType.DMA((COPIES,)),
            pltpu.SemaphoreType.DMA((COPIES,)),
        ]
        + [pltpu.VMEM((3, SLOTS, size), bf16) for _, size in CHUNKS]
        + [pltpu.VMEM((4, SLOTS, size), bf16) for _, size in CHUNKS]
        + [pltpu.VMEM((4, 128, size), bf16) for _, size in CHUNKS]
        + [pltpu.VMEM((3, 128, size), bf16) for _, size in CHUNKS]
        + [pltpu.VMEM((64, 16, size), bf16) for _, size in CHUNKS],
        compiler_params=pltpu.CompilerParams(
            collective_id=0, has_side_effects=True, vmem_limit_bytes=60 * 1024 * 1024
        ),
        name="joint",
    )(table, lengths, frames, blocks, value_weight, gate_weight, out_weight, taps, gain)


def routing(block_device, block_sub, block_rows):
    tm, te, dp = places()
    first = (tm // 4) * 4
    devices = lax.dynamic_slice_in_dim(block_device.reshape(16, 64), first, 4, 0)
    subs = lax.dynamic_slice_in_dim(block_sub.reshape(16, 64), first, 4, 0)
    counts = lax.dynamic_slice_in_dim(block_rows.reshape(16, 64), tm, 1, 0)
    earlier = jnp.arange(64)[:, None] > jnp.arange(64)[None, :]
    column = devices % 4
    same = (column[:, :, None] == column[:, None, :]) & earlier[None]
    rank = jnp.sum(same.astype(jnp.int32), axis=2)
    slot = column * 20 + rank
    own = lax.dynamic_slice_in_dim(slot, tm % 4, 1, 0)
    own_hot = own == jnp.arange(80, dtype=jnp.int32)[:, None]
    source = jnp.sum(jnp.where(own_hot, jnp.arange(64, dtype=jnp.int32)[None], 0), axis=1)
    live = jnp.sum(jnp.where(own_hot, jnp.clip(counts - te * 16, 0, 16), 0), axis=1)
    place = (tm % 4) * 20 + jnp.arange(20, dtype=jnp.int32)
    hot = slot[:, None, :] == place[None, :, None]
    block = (devices // 4) * 8 + subs
    dest = jnp.sum(jnp.where(hot, block[:, None, :] + 1, 0), axis=2).reshape(80) - 1
    return jnp.concatenate([source, live, jnp.where(dest < 0, 64, dest)])


def on_device(
    inputs,
    grad_blocks,
    block_device,
    block_sub,
    block_rows,
    seg_lengths,
    value_weight,
    gate_weight,
    out_weight,
    conv_kernel,
    norm_gain,
):
    width = inputs.shape[2]
    input_grad, value_grad, gate_grad, out_grad, kernel_grad, gain_grad = joint_call(
        routing(block_device, block_sub, block_rows),
        seg_lengths,
        inputs[0],
        grad_blocks[0],
        value_weight,
        gate_weight,
        out_weight,
        conv_kernel,
        norm_gain[None],
    )
    return (
        input_grad[None],
        value_grad,
        gate_grad,
        out_grad,
        kernel_grad,
        gain_grad.reshape(width),
    )


def solution(mesh):
    in_specs = (
        P("dp", "tm", None),
        P("dp", "tm", "tensor", None),
        P("dp", None, None),
        P("dp", None),
        P("dp", None),
        P("dp", None),
        P("tensor", None),
        P("tensor", None),
        P("tensor", None),
        P(None, "tensor"),
        P(),
    )
    out_specs = (
        P("dp", ("tm", "tensor"), None),
        P("tensor", ("tm", "dp")),
        P("tensor", ("tm", "dp")),
        P("tensor", ("tm", "dp")),
        P(None, "tensor"),
        P(),
    )
    return jax.shard_map(
        on_device, mesh=mesh, in_specs=in_specs, out_specs=out_specs, check_vma=False
    )
```

time: 856 us -> 145 us (0.17)
  the two profiles are of different devices: /device:TPU:0 before, /device:TPU:1 now
where the time goes in v1:
time: 145 us
  Pallas kernels  127 us (88%)
  local copies, waits for them, and re-layouts  10.1 us (7%)
  other arithmetic  6.87 us (5%)
    pallas_call x1, Pallas kernels, joint_call(): pl.pallas_call(joint_kernel, out_shape=(jax.ShapeDtypeStruct((128, width)...  127 us
    unnamed x7, local copies, waits for them, and re-layouts  8.51 us
    unnamed x3, other arithmetic  4.04 us

profile of v1, /device:TPU:1, one launch (start us, length us, event | category | flops | bytes accessed | tf_op | source)
XLA Modules:
  0.0 144.8 jit_solution(16751976751476524522)
XLA Ops:
  0.7 0.5 broadcast.62
  1.2 1.3 reduce.11
  2.5 0.1 reshape.48
  2.6 1.3 reduce.10
  4.0 1.3 reduce.12
  5.3 0.1 reshape.49
  5.4 0.1 reshape.50
  5.5 1.3 broadcast_in_dim.59.gain_ref
  6.8 0.2 convert_reduce_fusion
  7.0 0.1 select_reduce_fusion.2
  7.1 0.5 select_reduce_fusion
  7.6 0.1 copy.28
  7.7 0.1 sub.27
  7.8 0.6 pad_add_fusion.table_ref
  8.5 127.1 %joint.1 = (bf16[128,1536]{1,0:T(8,128)(2,1)}, f32[192,48]{1,0:T(8,128)}, f32[192,48]{1,0:T(8,128)}, f32[192,48]{1,0:T(8,128)}, f32[31,192]{1,0:T(8,128)}, /*index=5*/f32[1,1536]{1,0:T(1,128)}) custom-call(s32[240]{0:T(256)} %pad_add_fusion.table_ref, s32[1,22]{1,0:T(1,128)} %lengths_ref.1, bf16[1024,1536]{1,0:T(8,128)(2,1)} %bitcast.8, ...), custom_call_target="tpu_custom_call" | custom-call | tf_op jit(solution)/shard_map/joint/pallas_call | solution.py:716
  135.6 1.3 reduce.3
  136.9 1.6 %copy.25 = f32[192,48]{0,1:T(8,128)} copy(f32[192,48]{1,0:T(8,128)} %get-tuple-element.31) | data formatting | bytes 73728
  138.5 1.6 %copy.26 = f32[192,48]{0,1:T(8,128)} copy(f32[192,48]{1,0:T(8,128)} %get-tuple-element.32) | data formatting | bytes 73728
  140.1 1.6 %copy.27 = f32[192,48]{0,1:T(8,128)} copy(f32[192,48]{1,0:T(8,128)} %get-tuple-element.33) | data formatting | bytes 73728
  141.7 1.8 %copy.31 = bf16[1,128,1536]{2,1,0:T(8,128)(2,1)} copy(bf16[1,128,1536]{2,1,0:T(8,128)(2,1)} %bitcast.10) | data formatting | bytes 786432
  143.4 1.4 copy.32
  (7 shorter events, 0.1 us)

commit v2 on v1

--- a/solution.py
+++ b/solution.py
@@ -92,10 +92,10 @@
     return {"tm": (tm + step) % 16, "tensor": te, "dp": dp}
 
 
-CHUNKS = ((0, 512), (512, 512), (1024, 256), (1280, 256))
+CHUNKS = tuple((first, 256) for first in range(0, 1536, 256))
 HALVES = ((0, 768), (768, 768))
 SLOTS = 320
-COPIES = 13 * len(CHUNKS) + 4 + 7 * len(HALVES) + 12 + 14 + 7 + 3 + 7
+COPIES = 16 * len(CHUNKS) + 4 + 7 * len(HALVES) + 18 + 21 + 7 + 3 + 7
 
 
 def joint_kernel(
@@ -109,11 +109,10 @@
     taps_ref,
     gain_ref,
     input_grad,
-    value_grad,
-    gate_grad,
-    out_grad,
-    kernel_grad,
-    gain_grad,
+    wide_sum,
+    tail_sum,
+    out_sum,
+    small_sum,
     frames_ref,
     pair_ref,
     last_ref,
@@ -146,13 +145,20 @@
     x_b,
     x_plus,
     x_minus,
-    both_ref,
-    both_a,
-    both_b,
-    both_plus,
-    both_minus,
-    both_mid,
-    both_z,
+    wide_ref,
+    wide_a,
+    wide_b,
+    wide_plus,
+    wide_minus,
+    wide_mid,
+    wide_z,
+    tail_ref,
+    tail_a,
+    tail_b,
+    tail_plus,
+    tail_minus,
+    tail_mid,
+    tail_z,
     out_ref,
     out_a,
     out_b,
@@ -174,13 +180,15 @@
     count = len(CHUNKS)
     y_out, y_in = (rest[:count], rest[count : 2 * count])
     z_out, z_in = (rest[2 * count : 3 * count], rest[3 * count : 4 * count])
-    blocks = rest[4 * count :]
+    blocks, z_pass = (rest[4 * count : 5 * count], rest[5 * count :])
     tm, te, dp = places()
     y, zh, z = (tm % 4, tm // 4, (tm // 4) * 2 + dp)
     x, core = (te // 2, te % 2)
     bf16 = jnp.bfloat16
     factor = 1.0 / math.sqrt(32768.0)
     columns = [pl.ds(first, size) for first, size in CHUNKS]
+    half_a, half_b = (pl.ds(0, 64), pl.ds(64, 64))
+    zh_next, zh_last, zh_far = ((zh + 1) % 4, (zh + 3) % 4, (zh + 2) % 4)
 
     loads = []
 
@@ -245,18 +253,27 @@
             for at in range(4):
                 z_out[c][at, :, cols] = total[128 * at : 128 * at + 128]
 
-        return [
-            net.send(z_out[c].at[(zh + k) % 4], z_in[c].at[k - 1], z_peer(2 * k))
-            for k in (2, 1, 3)
-        ]
+        sums, passing = (z_out[c], z_pass[c])
+        return (
+            net.send(sums.at[zh_far, half_a], passing.at[0], z_peer(2)),
+            net.send(sums.at[zh_far, half_b], passing.at[1], z_peer(-2)),
+            net.send(sums.at[zh_next, half_b], z_in[c].at[0, half_b], z_peer(2)),
+            net.send(sums.at[zh_last, half_a], z_in[c].at[1, half_a], z_peer(-2)),
+        )
+
+    def forward(c, copies):
+        sums, passing = (z_out[c], z_pass[c])
+        copies[0].wait_recv()
+        passing[0] = (f32(passing[0]) + f32(sums[zh_next, half_a])).astype(bf16)
+        one = net.send(passing.at[0], z_in[c].at[0, half_a], z_peer(2))
+        copies[1].wait_recv()
+        passing[1] = (f32(passing[1]) + f32(sums[zh_last, half_b])).astype(bf16)
+        return copies[2:] + (one, net.send(passing.at[1], z_in[c].at[1, half_b], z_peer(-2)))
 
     def spread(c, copies):
         for copy in copies:
             copy.wait_recv()
-        total = f32(z_out[c][zh])
-        for k in range(3):
-            total = total + f32(z_in[c][k])
-        total = total.astype(bf16)
+        total = (f32(z_out[c][zh]) + f32(z_in[c][0]) + f32(z_in[c][1])).astype(bf16)
         for block in range(8):
             full_ref[block, te, :, columns[c]] = total[16 * block : 16 * block + 16]
         own = full_ref.at[:, te, :, columns[c]]
@@ -287,7 +304,7 @@
             else:
                 cot_ref[rows] += term
 
-    y_copies = [place(0), place(1)]
+    y_copies = [place(0), place(1), place(2)]
 
     @pl.loop(0, 10)
     def _(group):
@@ -313,6 +330,9 @@
 
     for copy in weight_loads:
         copy.wait()
+
+    z_copies = [combine(0, y_copies[0])]
+    y_copies.append(place(3))
 
     @pl.loop(0, 1024, step=256)
     def _(row):
@@ -337,8 +357,9 @@
         net.send(edge_out.at[1], edge_in.at[0], frame_peer(1)),
     )
 
-    z_copies = [combine(0, y_copies[0])]
-    y_copies.append(place(2))
+    z_copies.append(combine(1, y_copies[1]))
+    y_copies.append(place(4))
+    z_passed = [forward(0, z_copies[0])]
 
     taps[...] = jnp.zeros(taps.shape, jnp.float32)
     taps[:KERNEL, :192] = f32(taps_ref[...])
@@ -386,22 +407,20 @@
         swish_ref[rows, 128:] = (total_1 * jax.nn.sigmoid(total_1)).astype(bf16)
 
     out_load.wait()
-    z_copies.append(combine(1, y_copies[1]))
-    y_copies.append(place(3))
-    x_copies = [spread(0, z_copies[0])]
-    z_copies.append(combine(2, y_copies[2]))
-    x_copies.append(spread(1, z_copies[1]))
-    last = [relay(0, x_copies[0])]
-    project(0, last[0])
-    z_copies.append(combine(3, y_copies[3]))
-    x_copies.append(spread(2, z_copies[2]))
-    last.append(relay(1, x_copies[1]))
-    project(1, last[1])
-    x_copies.append(spread(3, z_copies[3]))
-    last.append(relay(2, x_copies[2]))
-    project(2, last[2])
-    last.append(relay(3, x_copies[3]))
-    project(3, last[3])
+    x_copies, last = ([], [])
+    for c in range(2, count + 4):
+        if c < count:
+            z_copies.append(combine(c, y_copies[c]))
+            if len(y_copies) < count:
+                y_copies.append(place(len(y_copies)))
+        if c - 1 < count:
+            z_passed.append(forward(c - 1, z_copies[c - 1]))
+        if c - 2 < count:
+            x_copies.append(spread(c - 2, z_passed[c - 2]))
+        if 0 <= c - 3 < count:
+            last.append(relay(c - 3, x_copies[c - 3]))
+        if 0 <= c - 4 < count:
+            project(c - 4, last[c - 4])
 
     @pl.loop(0, 1024, step=64)
     def _(row):
@@ -481,7 +500,8 @@
             out_ref[at, k] = term[96 * k : 96 * k + 96]
 
     out_set = (out_a, out_b, out_plus, out_minus)
-    both_set = (both_a, both_b, both_plus, both_minus)
+    wide_set = (wide_a, wide_b, wide_plus, wide_minus)
+    tail_set = (tail_a, tail_b, tail_plus, tail_minus)
     out_begun = begin_y(out_ref, *out_set)
 
     for at, first in ((0, 0), (1, 1040)):
@@ -489,41 +509,60 @@
         cot_0[first : first + 16] = far_in[at, :, :128]
         cot_1[first : first + 16] = far_in[at, :, 128:]
 
-    def back(row):
+    def back(row, lanes, cot, glu):
         rows = pl.ds(pl.multiple_of(row, 32), 32)
         wide = pl.ds(pl.multiple_of(row + 16, 16), 32)
         ahead, behind = (ahead_ref[rows], behind_ref[rows])
-        here_0, here_1 = (cot_0[wide], cot_1[wide])
-        total_0 = jnp.zeros((32, 128), jnp.float32)
-        total_1 = jnp.zeros((32, 128), jnp.float32)
+        here = cot[wide]
+        total = jnp.zeros((32, 128), jnp.float32)
         for k in range(KERNEL):
             off = k - KERNEL // 2
             near = nearby(ahead, behind, off)
             shifted = pl.ds(row + 16 + off, 32)
             m = KERNEL - 1 - k
-            total_0 = total_0 + taps[m : m + 1, :128] * jnp.where(near, cot_0[shifted], 0.0)
-            total_1 = total_1 + taps[m : m + 1, 128:] * jnp.where(near, cot_1[shifted], 0.0)
-            term_0 = here_0 * jnp.where(near, glu_0[shifted], 0.0)
-            term_1 = here_1 * jnp.where(near, glu_1[shifted], 0.0)
-            tap_sums[k, :, :128] += jnp.sum(term_0.reshape(4, 8, 128), axis=0)
-            tap_sums[k, :, 128:] += jnp.sum(term_1.reshape(4, 8, 128), axis=0)
-        value_0, value_1 = (lin_ref[rows, :128], lin_ref[rows, 128:])
-        sig_0, sig_1 = (sig_ref[rows, :128], sig_ref[rows, 128:])
-        both_cot[rows, :128] = (total_0 * sig_0).astype(bf16)
-        both_cot[rows, 128:256] = (total_0 * value_0 * sig_0 * (1.0 - sig_0)).astype(bf16)
-        gate_1 = total_1 * value_1 * sig_1 * (1.0 - sig_1)
-        both_cot[rows, 256:] = (total_1 * sig_1 + pltpu.roll(gate_1, 64, 1)).astype(bf16)
+            total = total + taps[m : m + 1, lanes] * jnp.where(near, cot[shifted], 0.0)
+            term = here * jnp.where(near, glu[shifted], 0.0)
+            tap_sums[k, :, lanes] += jnp.sum(term.reshape(4, 8, 128), axis=0)
+        value, sig = (lin_ref[rows, lanes], sig_ref[rows, lanes])
+        return rows, total * sig, total * value * sig * (1.0 - sig)
+
+    @pl.loop(0, 1024, step=32)
+    def _(row):
+        rows, value_cot, gate_cot = back(row, slice(0, 128), cot_0, glu_0)
+        both_cot[rows, :128] = value_cot.astype(bf16)
+        both_cot[rows, 128:256] = gate_cot.astype(bf16)
+
+    out_passed = pass_y(out_begun, out_ref, *out_set)
+
+    @pl.loop(0, 4)
+    def _(at):
+        cols = pl.ds(pl.multiple_of(at * 384, 128), 384)
+        term = lax.dot_general(
+            norm_ref[:, cols],
+            both_cot[:, :256],
+            over_frames,
+            preferred_element_type=jnp.float32,
+        ).astype(bf16)
+        for k in range(4):
+            wide_ref[at, k] = term[96 * k : 96 * k + 96]
+
+    wide_begun = begin_y(wide_ref, *wide_set)
+
+    def back_tail(row):
+        rows, value_cot, gate_cot = back(row, slice(128, 256), cot_1, glu_1)
+        both_cot[rows, 256:] = (value_cot + pltpu.roll(gate_cot, 64, 1)).astype(bf16)
 
     @pl.loop(0, 512, step=32)
     def _(row):
-        back(row)
-
-    out_passed = pass_y(out_begun, out_ref, *out_set)
+        back_tail(row)
+
+    out_z_copies = begin_z(out_passed, out_ref, out_plus, out_minus, out_mid, out_z)
 
     @pl.loop(512, 1024, step=32)
     def _(row):
-        back(row)
-
+        back_tail(row)
+
+    wide_passed = pass_y(wide_begun, wide_ref, *wide_set)
     gain_sums[...] = jnp.zeros(gain_sums.shape, jnp.float32)
     core_copies = []
     for at, (first, size) in enumerate(HALVES):
@@ -552,12 +591,15 @@
     def _(at):
         cols = pl.ds(pl.multiple_of(at * 384, 128), 384)
         term = lax.dot_general(
-            norm_ref[:, cols], both_cot[...], over_frames, preferred_element_type=jnp.float32
+            norm_ref[:, cols],
+            both_cot[:, 256:],
+            over_frames,
+            preferred_element_type=jnp.float32,
         ).astype(bf16)
         for k in range(4):
-            both_ref[at, k] = term[96 * k : 96 * k + 96]
-
-    both_begun = begin_y(both_ref, *both_set)
+            tail_ref[at, k] = term[96 * k : 96 * k + 96]
+
+    tail_begun = begin_y(tail_ref, *tail_set)
 
     gain_rows = pl.ds(32, 8)
     small_ref[...] = jnp.zeros(small_ref.shape, jnp.float32)
@@ -571,7 +613,6 @@
         net.send(small_ref.at[gain_rows], gain_in.at[te], t_peer(k)) for k in range(1, 8)
     ]
 
-    half_a, half_b = (pl.ds(0, 64), pl.ds(64, 64))
     x_begun = []
     for at, (first, size) in enumerate(HALVES):
         core_copies[at].wait_recv()
@@ -598,8 +639,8 @@
         )
         x_begun.append((begun, plain))
 
-    out_z_copies = begin_z(out_passed, out_ref, out_plus, out_minus, out_mid, out_z)
-    both_passed = pass_y(both_begun, both_ref, *both_set)
+    wide_z_copies = begin_z(wide_passed, wide_ref, wide_plus, wide_minus, wide_mid, wide_z)
+    tail_passed = pass_y(tail_begun, tail_ref, *tail_set)
 
     x_passed = []
     for at, (first, size) in enumerate(HALVES):
@@ -634,7 +675,7 @@
     small_y[y] = small_mid[...]
     small_copies = [net.send(small_mid, small_y.at[y], y_peer(k)) for k in range(1, 4)]
 
-    both_z_copies = begin_z(both_passed, both_ref, both_plus, both_minus, both_mid, both_z)
+    tail_z_copies = begin_z(tail_passed, tail_ref, tail_plus, tail_minus, tail_mid, tail_z)
 
     for copy in small_copies:
         copy.wait_recv()
@@ -645,7 +686,8 @@
     small_z[z] = total
     last_copies = [net.send(small_last, small_z.at[z], z_peer(k)) for k in range(1, 8)]
 
-    out_grad[...] = end_z(out_z_copies, out_z).T[:192]
+    out_sum[...] = end_z(out_z_copies, out_z)
+    wide_sum[...] = end_z(wide_z_copies, wide_z)
 
     for copies in x_passed:
         for copy in copies:
@@ -675,22 +717,14 @@
             )
         ).astype(bf16)
 
-    both_sum = end_z(both_z_copies, both_z)
-    tail = both_sum[:, 256:].T
-    value_grad[:128] = both_sum[:, :128].T
-    gate_grad[:128] = both_sum[:, 128:256].T
-    value_grad[128:] = tail[:64]
-    gate_grad[128:] = tail[64:]
+    tail_sum[...] = end_z(tail_z_copies, tail_z)
 
     for copy in last_copies:
         copy.wait_recv()
     total = small_z[0]
     for at in range(1, 8):
         total = total + small_z[at]
-    total = total * factor
-    kernel_grad[...] = total[:KERNEL, :192]
-    for k in range(6):
-        gain_grad[:, 256 * k : 256 * k + 256] = total[32 + k : 33 + k]
+    small_sum[...] = total * factor
     net.finish()
 
 
@@ -717,14 +751,13 @@
         joint_kernel,
         out_shape=(
             jax.ShapeDtypeStruct((128, width), bf16),
-            jax.ShapeDtypeStruct((span, 48), single),
-            jax.ShapeDtypeStruct((span, 48), single),
-            jax.ShapeDtypeStruct((span, 48), single),
-            jax.ShapeDtypeStruct((KERNEL, span), single),
-            jax.ShapeDtypeStruct((1, width), single),
+            jax.ShapeDtypeStruct((48, 256), single),
+            jax.ShapeDtypeStruct((48, 128), single),
+            jax.ShapeDtypeStruct((48, 256), single),
+            jax.ShapeDtypeStruct((40, 256), single),
         ),
-        in_specs=[smem, smem] + [where] * 5 + [vmem] * 2,
-        out_specs=[vmem] * 6,
+        in_specs=[smem] * 2 + [where] * 5 + [vmem] * 2,
+        out_specs=[vmem] * 5,
         scratch_shapes=[
             pltpu.VMEM((count, width), bf16),
             pltpu.VMEM((2 * span, width), bf16),
@@ -759,7 +792,8 @@
             pltpu.VMEM((128, width), bf16),
             pltpu.VMEM((128, width), bf16),
         ]
-        + weight_scratch(2 * span)
+        + weight_scratch(256)
+        + weight_scratch(128)
         + weight_scratch(256)
         + [
             pltpu.VMEM((40, 256), single),
@@ -775,13 +809,57 @@
         + [pltpu.VMEM((3, SLOTS, size), bf16) for _, size in CHUNKS]
         + [pltpu.VMEM((4, SLOTS, size), bf16) for _, size in CHUNKS]
         + [pltpu.VMEM((4, 128, size), bf16) for _, size in CHUNKS]
-        + [pltpu.VMEM((3, 128, size), bf16) for _, size in CHUNKS]
-        + [pltpu.VMEM((64, 16, size), bf16) for _, size in CHUNKS],
+        + [pltpu.VMEM((2, 128, size), bf16) for _, size in CHUNKS]
+        + [pltpu.VMEM((64, 16, size), bf16) for _, size in CHUNKS]
+        + [pltpu.VMEM((2, 64, size), bf16) for _, size in CHUNKS],
         compiler_params=pltpu.CompilerParams(
             collective_id=0, has_side_effects=True, vmem_limit_bytes=60 * 1024 * 1024
         ),
         name="joint",
     )(table, lengths, frames, blocks, value_weight, gate_weight, out_weight, taps, gain)
+
+
+def finish_kernel(
+    input_ref,
+    wide_ref,
+    tail_ref,
+    out_ref,
+    small_ref,
+    input_grad,
+    value_grad,
+    gate_grad,
+    out_grad,
+    kernel_grad,
+    gain_grad,
+):
+    input_grad[...] = input_ref[...]
+    tail = tail_ref[...]
+    value_grad[:, :128] = wide_ref[:, :128]
+    value_grad[:, 128:] = tail[:, :64]
+    gate_grad[:, :128] = wide_ref[:, 128:]
+    gate_grad[:, 128:] = pltpu.roll(tail, 64, 1)[:, :64]
+    out_grad[...] = out_ref[:, :192]
+    kernel_grad[...] = small_ref[:KERNEL, :192]
+    for k in range(6):
+        gain_grad[:, 256 * k : 256 * k + 256] = small_ref[32 + k : 33 + k]
+
+
+def finish_call(*sums):
+    single = jnp.float32
+    width = sums[0].shape[1]
+    vmem = pl.BlockSpec(memory_space=pltpu.VMEM)
+    return pl.pallas_call(
+        finish_kernel,
+        out_shape=(jax.ShapeDtypeStruct(sums[0].shape, jnp.bfloat16),)
+        + (jax.ShapeDtypeStruct((48, 192), single),) * 3
+        + (
+            jax.ShapeDtypeStruct((KERNEL, 192), single),
+            jax.ShapeDtypeStruct((1, width), single),
+        ),
+        in_specs=[vmem] * 5,
+        out_specs=[vmem] * 6,
+        name="finish",
+    )(*sums)
 
 
 def routing(block_device, block_sub, block_rows):
@@ -820,7 +898,7 @@
     norm_gain,
 ):
     width = inputs.shape[2]
-    input_grad, value_grad, gate_grad, out_grad, kernel_grad, gain_grad = joint_call(
+    sums = joint_call(
         routing(block_device, block_sub, block_rows),
         seg_lengths,
         inputs[0],
@@ -831,11 +909,12 @@
         conv_kernel,
         norm_gain[None],
     )
+    input_grad, value_grad, gate_grad, out_grad, kernel_grad, gain_grad = finish_call(*sums)
     return (
         input_grad[None],
-        value_grad,
-        gate_grad,
-        out_grad,
+        value_grad.T,
+        gate_grad.T,
+        out_grad.T,
         kernel_grad,
         gain_grad.reshape(width),
     )

time: 145 us -> 135 us (0.931); the launches traced: 145 us -> 133 us
  local copies, waits for them, and re-layouts: 10.1 us -> 2.19 us
  Pallas kernels: 127 us -> 123 us
    unnamed x7 -> x2, local copies, waits for them, and re-layouts: 8.51 us -> 0.6 us
    pallas_call x1, Pallas kernels: 127 us -> 121 us  [joint_call(): pl.pallas_call(joint_kernel, out_shape=(jax.ShapeDtypeStruct((128, width)...]
    pallas_call x0 -> x1, Pallas kernels: none -> 1.87 us  [finish_call(): pl.pallas_call(finish_kernel, out_shape=(jax.ShapeDtypeStruct(sums[0].sha...]
where the time goes in v2:
time: 135 us; the launch traced here: 133 us
  Pallas kernels  123 us (91%)
  other arithmetic  6.87 us (5%)
  local copies, waits for them, and re-layouts  2.19 us (2%)
    pallas_call x1, Pallas kernels, joint_call(): pl.pallas_call(joint_kernel, out_shape=(jax.ShapeDtypeStruct((128, width)...  121 us
    unnamed x3, other arithmetic  4.04 us

profile of v2, /device:TPU:1, one launch (start us, length us, event | category | flops | bytes accessed | tf_op | source)
XLA Modules:
  0.0 132.8 jit_solution(15065222833110281836)
XLA Ops:
  0.7 0.5 broadcast.62
  1.2 1.3 %reduce.11 = s32[1024]{0:T(1024)S(1)} reduce(s32[1,1024,1]{1,2,0:T(1,128)} %param.13, s32[]{:T(128)} %broadcast.62), dimensions={0,2}, to_apply=%param.13.reduce_sub_computation.3 | reduce | bytes 8196 | tf_op args[2]
  2.5 0.1 reshape.48
  2.6 1.3 %reduce.10 = s32[1024]{0:T(1024)S(1)} reduce(s32[1,1024]{1,0:T(1,128)} %param.14, s32[]{:T(128)} %broadcast.62), dimensions={0}, to_apply=%param.14.reduce_sub_computation.3 | reduce | bytes 8196 | tf_op args[3]
  4.0 1.3 %reduce.12 = s32[1024]{0:T(1024)S(1)} reduce(s32[1,1024]{1,0:T(1,128)} %param.15, s32[]{:T(128)} %broadcast.62), dimensions={0}, to_apply=%param.15.reduce_sub_computation.3 | reduce | bytes 8196 | tf_op args[4]
  5.3 0.1 reshape.49
  5.4 0.1 reshape.50
  5.5 1.3 broadcast_in_dim.59.gain_ref
  6.8 0.2 convert_reduce_fusion
  7.0 0.1 select_reduce_fusion.2
  7.1 0.5 select_reduce_fusion
  7.6 0.1 copy.19
  7.7 0.1 sub.27
  7.8 0.6 pad_add_fusion.table_ref
  8.5 121.2 %joint.1 = (bf16[128,1536]{1,0:T(8,128)(2,1)}, f32[48,256]{1,0:T(8,128)}, f32[48,128]{1,0:T(8,128)}, f32[48,256]{1,0:T(8,128)}, f32[40,256]{1,0:T(8,128)}) custom-call(s32[240]{0:T(256)} %pad_add_fusion.table_ref, s32[1,22]{1,0:T(1,128)} %lengths_ref.1, bf16[1024,1536]{1,0:T(8,128)(2,1)} %bitcast.11, bf16[64,16,1536]{2,1,0:T(8,128)(2,1)} %bitcast.12, ...), custom_call_target="tpu_custom_call" | custom-call | tf_op jit(solution)/shard_map/joint/pallas_call | solution.py:750
  129.6 1.9 %finish.1 = (bf16[128,1536]{1,0:T(8,128)(2,1)}, f32[48,192]{1,0:T(8,128)}, f32[48,192]{1,0:T(8,128)}, f32[48,192]{1,0:T(8,128)}, f32[31,192]{1,0:T(8,128)}, /*index=5*/f32[1,1536]{1,0:T(1,128)}) custom-call(bf16[128,1536]{1,0:T(8,128)(2,1)} %get-tuple-element.17.input_ref, f32[48,256]{1,0:T(8,128)} %get-tuple-element.18.wide_ref, ...), custom_call_target="tpu_custom_call" | custom-call | tf_op jit(solution)/shard_map/finish/pallas_call | solution.py:851
  131.5 1.3 reduce.3
  (7 shorter events, 0.1 us)

commit v3 on v2

--- a/solution.py
+++ b/solution.py
@@ -95,7 +95,7 @@
 CHUNKS = tuple((first, 256) for first in range(0, 1536, 256))
 HALVES = ((0, 768), (768, 768))
 SLOTS = 320
-COPIES = 16 * len(CHUNKS) + 4 + 7 * len(HALVES) + 18 + 21 + 7 + 3 + 7
+COPIES = 16 * len(CHUNKS) + 4 + 7 * len(HALVES) + 18 + 21 + 7 + 3 + 7 + 3 + 7
 
 
 def joint_kernel(
@@ -166,12 +166,19 @@
     out_minus,
     out_mid,
     out_z,
-    small_ref,
+    gain_row,
+    own_normed,
+    own_scale,
+    kern_ref,
+    kern_y,
+    kern_mid,
+    kern_z,
+    gain_out,
     gain_in,
-    small_mid,
-    small_y,
-    small_last,
-    small_z,
+    gain_mid,
+    gain_y,
+    gain_last,
+    gain_z,
     load_sems,
     send_sems,
     recv_sems,
@@ -190,6 +197,8 @@
     half_a, half_b = (pl.ds(0, 64), pl.ds(64, 64))
     zh_next, zh_last, zh_far = ((zh + 1) % 4, (zh + 3) % 4, (zh + 2) % 4)
 
+    for k in range(6):
+        gain_row[:, 256 * k : 256 * k + 256] = gain_ref[256 * k : 256 * k + 256].reshape(1, 256)
     loads = []
 
     def load(src, dst):
@@ -326,7 +335,7 @@
         cells = f32(frames_ref[rows])
         centered = cells - jnp.mean(cells, axis=1, keepdims=True)
         scale = lax.rsqrt(jnp.mean(centered * centered, axis=1, keepdims=True) + epsilon)
-        norm_ref[rows] = ((centered * scale) * gain_ref[...]).astype(bf16)
+        norm_ref[rows] = ((centered * scale) * gain_row[...]).astype(bf16)
 
     for copy in weight_loads:
         copy.wait()
@@ -360,6 +369,15 @@
     z_copies.append(combine(1, y_copies[1]))
     y_copies.append(place(4))
     z_passed = [forward(0, z_copies[0])]
+
+    @pl.loop(0, 128, step=32)
+    def _(row):
+        rows = pl.ds(pl.multiple_of(row, 32), 32)
+        cells = f32(frames_ref[pl.ds(pl.multiple_of(te * 128 + row, 32), 32)])
+        centered = cells - jnp.mean(cells, axis=1, keepdims=True)
+        scale = lax.rsqrt(jnp.mean(centered * centered, axis=1, keepdims=True) + epsilon)
+        own_normed[rows] = centered * scale
+        own_scale[rows] = jnp.broadcast_to(scale, (32, 128))
 
     taps[...] = jnp.zeros(taps.shape, jnp.float32)
     taps[:KERNEL, :192] = f32(taps_ref[...])
@@ -563,9 +581,26 @@
         back_tail(row)
 
     wide_passed = pass_y(wide_begun, wide_ref, *wide_set)
+    kern_ref[...] = jnp.zeros(kern_ref.shape, jnp.float32)
+    for k in range(KERNEL):
+        kern_ref[k : k + 1] = jnp.sum(tap_sums[k], axis=0, keepdims=True)
+    kern_y[y] = kern_ref[...]
+    kern_copies = [net.send(kern_ref, kern_y.at[y], y_peer(k)) for k in (2, 1, 3)]
+
+    def shares(refs, copies):
+        for copy in copies:
+            copy.wait_recv()
+        total = refs[0]
+        for at in range(1, refs.shape[0]):
+            total = total + refs[at]
+        return total
+
     gain_sums[...] = jnp.zeros(gain_sums.shape, jnp.float32)
     core_copies = []
-    for at, (first, size) in enumerate(HALVES):
+
+    def norm_part(at):
+        first, size = HALVES[at]
+
         @pl.loop(first, first + size, step=256)
         def _(col):
             cols = pl.ds(pl.multiple_of(col, 256), 256)
@@ -587,6 +622,65 @@
             net.send(part_ref.at[:, 1 - core, :, cols], core_in.at[:, :, cols], sibling())
         )
 
+    def begin_x(at):
+        core_copies[at].wait_recv()
+        first, size = HALVES[at]
+        cols = pl.ds(first, size)
+
+        def add_core(to):
+            @pl.loop(0, 128, step=32)
+            def _(row):
+                rows = pl.ds(pl.multiple_of(row, 32), 32)
+                chip_sum[to, rows, cols] = (
+                    f32(part_ref[to, core, rows, cols]) + f32(core_in[to, rows, cols])
+                ).astype(bf16)
+
+        add_core(x_far)
+        begun = (
+            net.send(chip_sum.at[x_far, half_a, cols], x_a.at[:, cols], x_peer(1)),
+            net.send(chip_sum.at[x_far, half_b, cols], x_b.at[:, cols], x_peer(-1)),
+        )
+        add_core(x_next)
+        add_core(x_last)
+        plain = (
+            net.send(chip_sum.at[x_next, half_b, cols], x_plus.at[half_b, cols], x_peer(1)),
+            net.send(chip_sum.at[x_last, half_a, cols], x_minus.at[half_a, cols], x_peer(-1)),
+        )
+        return begun, plain
+
+    def pass_x(at, pending):
+        begun, plain = pending
+        first, size = HALVES[at]
+        cols = pl.ds(first, size)
+
+        def add_x(ref, to, start):
+            @pl.loop(0, 64, step=32)
+            def _(row):
+                rows = pl.ds(pl.multiple_of(row, 32), 32)
+                other = pl.ds(pl.multiple_of(row + start, 32), 32)
+                ref[rows, cols] = (f32(ref[rows, cols]) + f32(chip_sum[to, other, cols])).astype(
+                    bf16
+                )
+
+        begun[0].wait_recv()
+        add_x(x_a, x_next, 0)
+        one = net.send(x_a.at[:, cols], x_plus.at[half_a, cols], x_peer(1))
+        begun[1].wait_recv()
+        add_x(x_b, x_last, 64)
+        return plain + (one, net.send(x_b.at[:, cols], x_minus.at[half_b, cols], x_peer(-1)))
+
+    norm_part(0)
+    norm_part(1)
+    x_begun = [begin_x(0)]
+
+    gain_ref_in = jnp.sum(gain_sums[...], axis=0, keepdims=True) / gain_row[...]
+    gain_out[...] = jnp.zeros(gain_out.shape, jnp.float32)
+    for k in range(6):
+        gain_out[k : k + 1] = gain_ref_in[:, 256 * k : 256 * k + 256]
+    gain_in[te] = gain_out[...]
+    gain_copies = [net.send(gain_out, gain_in.at[te], t_peer(k)) for k in range(1, 8)]
+    x_begun.append(begin_x(1))
+
     @pl.loop(0, 4)
     def _(at):
         cols = pl.ds(pl.multiple_of(at * 384, 128), 384)
@@ -600,94 +694,24 @@
             tail_ref[at, k] = term[96 * k : 96 * k + 96]
 
     tail_begun = begin_y(tail_ref, *tail_set)
-
-    gain_rows = pl.ds(32, 8)
-    small_ref[...] = jnp.zeros(small_ref.shape, jnp.float32)
-    for k in range(KERNEL):
-        small_ref[k : k + 1] = jnp.sum(tap_sums[k], axis=0, keepdims=True)
-    gain_part = jnp.sum(gain_sums[...], axis=0, keepdims=True) / gain_ref[...]
-    for k in range(6):
-        small_ref[32 + k : 33 + k] = gain_part[:, 256 * k : 256 * k + 256]
-    gain_in[te] = small_ref[gain_rows, :]
-    gain_copies = [
-        net.send(small_ref.at[gain_rows], gain_in.at[te], t_peer(k)) for k in range(1, 8)
-    ]
-
-    x_begun = []
-    for at, (first, size) in enumerate(HALVES):
-        core_copies[at].wait_recv()
-        cols = pl.ds(first, size)
-
-        def add_core(to):
-            @pl.loop(0, 128, step=32)
-            def _(row):
-                rows = pl.ds(pl.multiple_of(row, 32), 32)
-                chip_sum[to, rows, cols] = (
-                    f32(part_ref[to, core, rows, cols]) + f32(core_in[to, rows, cols])
-                ).astype(bf16)
-
-        add_core(x_far)
-        begun = (
-            net.send(chip_sum.at[x_far, half_a, cols], x_a.at[:, cols], x_peer(1)),
-            net.send(chip_sum.at[x_far, half_b, cols], x_b.at[:, cols], x_peer(-1)),
-        )
-        add_core(x_next)
-        add_core(x_last)
-        plain = (
-            net.send(chip_sum.at[x_next, half_b, cols], x_plus.at[half_b, cols], x_peer(1)),
-            net.send(chip_sum.at[x_last, half_a, cols], x_minus.at[half_a, cols], x_peer(-1)),
-        )
-        x_begun.append((begun, plain))
-
+    kern_mid[...] = shares(kern_y, kern_copies)
+    kern_z[z] = kern_mid[...]
+    kern_copies = [net.send(kern_mid, kern_z.at[z], z_peer(k)) for k in (4, 3, 5, 2, 6, 1, 7)]
     wide_z_copies = begin_z(wide_passed, wide_ref, wide_plus, wide_minus, wide_mid, wide_z)
+    gain_mid[...] = shares(gain_in, gain_copies)
+    gain_y[y] = gain_mid[...]
+    gain_copies = [net.send(gain_mid, gain_y.at[y], y_peer(k)) for k in (2, 1, 3)]
+    x_passed = [pass_x(0, x_begun[0])]
     tail_passed = pass_y(tail_begun, tail_ref, *tail_set)
-
-    x_passed = []
-    for at, (first, size) in enumerate(HALVES):
-        begun, plain = x_begun[at]
-        cols = pl.ds(first, size)
-
-        def add_x(ref, to, start):
-            @pl.loop(0, 64, step=32)
-            def _(row):
-                rows = pl.ds(pl.multiple_of(row, 32), 32)
-                other = pl.ds(pl.multiple_of(row + start, 32), 32)
-                ref[rows, cols] = (f32(ref[rows, cols]) + f32(chip_sum[to, other, cols])).astype(
-                    bf16
-                )
-
-        begun[0].wait_recv()
-        add_x(x_a, x_next, 0)
-        one = net.send(x_a.at[:, cols], x_plus.at[half_a, cols], x_peer(1))
-        begun[1].wait_recv()
-        add_x(x_b, x_last, 64)
-        x_passed.append(
-            plain + (one, net.send(x_b.at[:, cols], x_minus.at[half_b, cols], x_peer(-1)))
-        )
-
-    for copy in gain_copies:
-        copy.wait_recv()
-    small_mid[pl.ds(0, 32), :] = small_ref[pl.ds(0, 32), :]
-    total = gain_in[0]
-    for at in range(1, 8):
-        total = total + gain_in[at]
-    small_mid[gain_rows, :] = total
-    small_y[y] = small_mid[...]
-    small_copies = [net.send(small_mid, small_y.at[y], y_peer(k)) for k in range(1, 4)]
-
+    x_passed.append(pass_x(1, x_begun[1]))
+    gain_last[...] = shares(gain_y, gain_copies)
+    gain_z[z] = gain_last[...]
+    gain_copies = [net.send(gain_last, gain_z.at[z], z_peer(k)) for k in (4, 3, 5, 2, 6, 1, 7)]
     tail_z_copies = begin_z(tail_passed, tail_ref, tail_plus, tail_minus, tail_mid, tail_z)
-
-    for copy in small_copies:
-        copy.wait_recv()
-    total = small_y[0]
-    for at in range(1, 4):
-        total = total + small_y[at]
-    small_last[...] = total
-    small_z[z] = total
-    last_copies = [net.send(small_last, small_z.at[z], z_peer(k)) for k in range(1, 8)]
 
     out_sum[...] = end_z(out_z_copies, out_z)
     wide_sum[...] = end_z(wide_z_copies, wide_z)
+    small_sum[pl.ds(0, 32), :] = shares(kern_z, kern_copies) * factor
 
     for copies in x_passed:
         for copy in copies:
@@ -702,14 +726,11 @@
             + f32(x_plus[rows])
             + f32(x_minus[rows])
         )
-        cells = f32(frames_ref[pl.ds(pl.multiple_of(te * 128 + block * 16, 16), 16)])
-        centered = cells - jnp.mean(cells, axis=1, keepdims=True)
-        inv_std = lax.rsqrt(jnp.mean(centered * centered, axis=1, keepdims=True) + epsilon)
-        normed = centered * inv_std
-        scaled = summed * gain_ref[...]
+        normed = own_normed[rows]
+        scaled = summed * gain_row[...]
         input_grad[rows] = (
             f32(full_ref[te, block])
-            + inv_std
+            + own_scale[rows, :1]
             * (
                 scaled
                 - jnp.mean(scaled, axis=1, keepdims=True)
@@ -718,13 +739,7 @@
         ).astype(bf16)
 
     tail_sum[...] = end_z(tail_z_copies, tail_z)
-
-    for copy in last_copies:
-        copy.wait_recv()
-    total = small_z[0]
-    for at in range(1, 8):
-        total = total + small_z[at]
-    small_sum[...] = total * factor
+    small_sum[pl.ds(32, 8), :] = shares(gain_z, gain_copies) * factor
     net.finish()
 
 
@@ -796,12 +811,19 @@
         + weight_scratch(128)
         + weight_scratch(256)
         + [
-            pltpu.VMEM((40, 256), single),
+            pltpu.VMEM((1, width), single),
+            pltpu.VMEM((128, width), single),
+            pltpu.VMEM((128, 128), single),
+            pltpu.VMEM((32, 256), single),
+            pltpu.VMEM((4, 32, 256), single),
+            pltpu.VMEM((32, 256), single),
+            pltpu.VMEM((8, 32, 256), single),
+            pltpu.VMEM((8, 256), single),
             pltpu.VMEM((8, 8, 256), single),
-            pltpu.VMEM((40, 256), single),
-            pltpu.VMEM((4, 40, 256), single),
-            pltpu.VMEM((40, 256), single),
-            pltpu.VMEM((8, 40, 256), single),
+            pltpu.VMEM((8, 256), single),
+            pltpu.VMEM((4, 8, 256), single),
+            pltpu.VMEM((8, 256), single),
+            pltpu.VMEM((8, 8, 256), single),
             pltpu.SemaphoreType.DMA((len(CHUNKS) + 6,)),
             pltpu.SemaphoreType.DMA((COPIES,)),
             pltpu.SemaphoreType.DMA((COPIES,)),
@@ -841,7 +863,7 @@
     out_grad[...] = out_ref[:, :192]
     kernel_grad[...] = small_ref[:KERNEL, :192]
     for k in range(6):
-        gain_grad[:, 256 * k : 256 * k + 256] = small_ref[32 + k : 33 + k]
+        gain_grad[256 * k : 256 * k + 256] = small_ref[32 + k]
 
 
 def finish_call(*sums):
@@ -854,7 +876,7 @@
         + (jax.ShapeDtypeStruct((48, 192), single),) * 3
         + (
             jax.ShapeDtypeStruct((KERNEL, 192), single),
-            jax.ShapeDtypeStruct((1, width), single),
+            jax.ShapeDtypeStruct((width,), single),
         ),
         in_specs=[vmem] * 5,
         out_specs=[vmem] * 6,
@@ -865,9 +887,11 @@
 def routing(block_device, block_sub, block_rows):
     tm, te, dp = places()
     first = (tm // 4) * 4
-    devices = lax.dynamic_slice_in_dim(block_device.reshape(16, 64), first, 4, 0)
-    subs = lax.dynamic_slice_in_dim(block_sub.reshape(16, 64), first, 4, 0)
-    counts = lax.dynamic_slice_in_dim(block_rows.reshape(16, 64), tm, 1, 0)
+    code = block_device.reshape(1, 1024) + 16 * block_sub + 128 * block_rows
+    code = code.reshape(16, 64)
+    near = lax.dynamic_slice_in_dim(code, first, 4, 0)
+    devices, subs = (near % 16, (near // 16) % 8)
+    counts = lax.dynamic_slice_in_dim(code, tm, 1, 0) // 128
     earlier = jnp.arange(64)[:, None] > jnp.arange(64)[None, :]
     column = devices % 4
     same = (column[:, :, None] == column[:, None, :]) & earlier[None]
@@ -897,7 +921,6 @@
     conv_kernel,
     norm_gain,
 ):
-    width = inputs.shape[2]
     sums = joint_call(
         routing(block_device, block_sub, block_rows),
         seg_lengths,
@@ -907,7 +930,7 @@
         gate_weight,
         out_weight,
         conv_kernel,
-        norm_gain[None],
+        norm_gain,
     )
     input_grad, value_grad, gate_grad, out_grad, kernel_grad, gain_grad = finish_call(*sums)
     return (
@@ -916,7 +939,7 @@
         gate_grad.T,
         out_grad.T,
         kernel_grad,
-        gain_grad.reshape(width),
+        gain_grad,
     )
 
 

time: 135 us -> 125 us (0.926); the launches traced: 133 us -> 125 us
  other arithmetic: 6.87 us -> 2.27 us
  local copies, waits for them, and re-layouts: 2.19 us -> 0.24 us
    unnamed x3 -> x0, other arithmetic: 4.04 us -> none
where the time goes in v3:
time: 125 us
  Pallas kernels  122 us (98%)
  other arithmetic  2.27 us (2%)
    pallas_call x1, Pallas kernels, joint_call(): pl.pallas_call(joint_kernel, out_shape=(jax.ShapeDtypeStruct((128, width)...  120 us

profile of v3, /device:TPU:1, one launch (start us, length us, event | category | flops | bytes accessed | tf_op | source)
XLA Modules:
  0.0 125.1 jit_solution(7826224333786739281)
XLA Ops:
  0.7 0.7 fusion.1
  1.4 0.1 reshape.43
  1.5 0.2 convert_reduce_fusion
  1.8 0.1 select_reduce_fusion.2
  1.9 0.5 select_reduce_fusion
  2.4 0.1 copy.19
  2.5 0.1 sub.39
  2.6 0.6 pad_add_fusion.table_ref
  3.2 120.0 %joint.1 = (bf16[128,1536]{1,0:T(8,128)(2,1)}, f32[48,256]{1,0:T(8,128)}, f32[48,128]{1,0:T(8,128)}, f32[48,256]{1,0:T(8,128)}, f32[40,256]{1,0:T(8,128)}) custom-call(s32[240]{0:T(256)} %pad_add_fusion.table_ref, s32[1,22]{1,0:T(1,128)} %lengths_ref.1, bf16[1024,1536]{1,0:T(8,128)(2,1)} %bitcast.16, bf16[64,16,1536]{2,1,0:T(8,128)(2,1)} %bitcast.17, ...), custom_call_target="tpu_custom_call" | custom-call | tf_op jit(solution)/shard_map/joint/pallas_call | solution.py:765
  123.2 1.9 %finish.1 = (bf16[128,1536]{1,0:T(8,128)(2,1)}, f32[48,192]{1,0:T(8,128)}, f32[48,192]{1,0:T(8,128)}, f32[48,192]{1,0:T(8,128)}, f32[31,192]{1,0:T(8,128)}, /*index=5*/f32[1536]{0:T(1024)}) custom-call(bf16[128,1536]{1,0:T(8,128)(2,1)} %get-tuple-element.17.input_ref, f32[48,256]{1,0:T(8,128)} %get-tuple-element.18.wide_ref, ...), custom_call_target="tpu_custom_call" | custom-call | tf_op jit(solution)/shard_map/finish/pallas_call | solution.py:873
  (7 shorter events, 0.1 us)

commit v4 on v3

--- a/solution.py
+++ b/solution.py
@@ -313,7 +313,7 @@
             else:
                 cot_ref[rows] += term
 
-    y_copies = [place(0), place(1), place(2)]
+    y_copies = [place(0), place(1)]
 
     @pl.loop(0, 10)
     def _(group):
@@ -341,7 +341,7 @@
         copy.wait()
 
     z_copies = [combine(0, y_copies[0])]
-    y_copies.append(place(3))
+    y_copies.append(place(2))
 
     @pl.loop(0, 1024, step=256)
     def _(row):
@@ -367,7 +367,7 @@
     )
 
     z_copies.append(combine(1, y_copies[1]))
-    y_copies.append(place(4))
+    y_copies.append(place(3))
     z_passed = [forward(0, z_copies[0])]
 
     @pl.loop(0, 128, step=32)

time: 125 us -> 122 us (0.976)
  Pallas kernels: 122 us -> 118 us
    pallas_call x1, Pallas kernels: 120 us -> 117 us  [joint_call(): pl.pallas_call(joint_kernel, out_shape=(jax.ShapeDtypeStruct((128, width)...]
where the time goes in v4:
time: 122 us
  Pallas kernels  118 us (97%)
  other arithmetic  2.27 us (2%)
    pallas_call x1, Pallas kernels, joint_call(): pl.pallas_call(joint_kernel, out_shape=(jax.ShapeDtypeStruct((128, width)...  117 us

profile of v4, /device:TPU:1, one launch (start us, length us, event | category | flops | bytes accessed | tf_op | source)
XLA Modules:
  0.0 121.7 jit_solution(10619030362940365170)
XLA Ops:
  0.7 0.7 fusion.1
  1.4 0.1 reshape.43
  1.5 0.2 convert_reduce_fusion
  1.8 0.1 select_reduce_fusion.2
  1.9 0.5 select_reduce_fusion
  2.4 0.1 copy.19
  2.5 0.1 sub.39
  2.6 0.6 pad_add_fusion.table_ref
  3.2 116.6 %joint.1 = (bf16[128,1536]{1,0:T(8,128)(2,1)}, f32[48,256]{1,0:T(8,128)}, f32[48,128]{1,0:T(8,128)}, f32[48,256]{1,0:T(8,128)}, f32[40,256]{1,0:T(8,128)}) custom-call(s32[240]{0:T(256)} %pad_add_fusion.table_ref, s32[1,22]{1,0:T(1,128)} %lengths_ref.1, bf16[1024,1536]{1,0:T(8,128)(2,1)} %bitcast.16, bf16[64,16,1536]{2,1,0:T(8,128)(2,1)} %bitcast.17, ...), custom_call_target="tpu_custom_call" | custom-call | tf_op jit(solution)/shard_map/joint/pallas_call | solution.py:765
  119.8 1.9 %finish.1 = (bf16[128,1536]{1,0:T(8,128)(2,1)}, f32[48,192]{1,0:T(8,128)}, f32[48,192]{1,0:T(8,128)}, f32[48,192]{1,0:T(8,128)}, f32[31,192]{1,0:T(8,128)}, /*index=5*/f32[1536]{0:T(1024)}) custom-call(bf16[128,1536]{1,0:T(8,128)(2,1)} %get-tuple-element.17.input_ref, f32[48,256]{1,0:T(8,128)} %get-tuple-element.18.wide_ref, ...), custom_call_target="tpu_custom_call" | custom-call | tf_op jit(solution)/shard_map/finish/pallas_call | solution.py:873
  (7 shorter events, 0.1 us)
